TPU v7x, 32 devices: a whole 2x2x4 slice. The times are simulated.
32 devices in a mesh: dp: 8 (over y, x, core), tensor: 4 (over z).
Axes of the slice: x: 2, y: 2, z: 4, core: 2. Of those that a mesh axis runs over, the one named last changes fastest.
Arguments:
- block_input: bfloat16 [24576, 768], P('dp'), may hold values from -6 to 6
- cotangent: bfloat16 [24576, 768], P('dp'), may hold values from -6 to 6
- heads_weight: bfloat16 [768, 2304], P('dp', 'tensor'), may hold values from -0.21875 to 0.21875
- heads_bias: bfloat16 [2304], P(('tensor', 'dp')), may hold values from -3 to 3
- merge_weight: bfloat16 [768, 768], P('tensor', 'dp'), may hold values from -0.875 to 0.875
- merge_bias: bfloat16 [768], P('dp'), may hold values from -3 to 3
- up_weight: bfloat16 [768, 3072], P('dp', 'tensor'), may hold values from -0.21875 to 0.21875
- up_bias: bfloat16 [3072], P(('tensor', 'dp')), may hold values from -3 to 3
- down_weight: bfloat16 [3072, 768], P('tensor', 'dp'), may hold values from -0.15625 to 0.15625
- down_bias: bfloat16 [768], P('dp'), may hold values from -3 to 3
- first_gain: bfloat16 [768], P('dp'), may hold values from 0.099609375 to 1.8984375
- first_shift: bfloat16 [768], P('dp'), may hold values from -2 to 2
- second_gain: bfloat16 [768], P('dp'), may hold values from 0.099609375 to 1.8984375
- second_shift: bfloat16 [768], P('dp'), may hold values from -2 to 2
Outputs:
- layer_output: bfloat16 [24576, 768], P('dp')
- input_grad: float32 [24576, 768], P('dp')
- heads_weight_grad: float32 [768, 2304], P('dp', 'tensor')
- heads_bias_grad: float32 [2304], P(('tensor', 'dp'))
- merge_weight_grad: float32 [768, 768], P('tensor', 'dp')
- merge_bias_grad: float32 [768], P('dp')
- up_weight_grad: float32 [768, 3072], P('dp', 'tensor')
- up_bias_grad: float32 [3072], P(('tensor', 'dp'))
- down_weight_grad: float32 [3072, 768], P('tensor', 'dp')
- down_bias_grad: float32 [768], P('dp')
- first_gain_grad: float32 [768], P('dp')
- first_shift_grad: float32 [768], P('dp')
- second_gain_grad: float32 [768], P('dp')
- second_shift_grad: float32 [768], P('dp')
All inputs are finite; a program needn't handle non-finite values.
Results may differ from a plain program's by a relative error of at most 0.012.
Values may be sent and summed in bfloat16 or wider, within the bound.
No kernel may reach another device: no remote copies, remote signals or barrier semaphores. Data moves between devices by JAX's collectives and lax.ppermute only.
A program may use at most 192 MiB of HBM per device.

v0:
```python
import functools
import math

import jax
import jax.numpy as jnp
import numpy as np
from jax import lax
from jax.experimental import pallas as pl
from jax.experimental.pallas import tpu as pltpu
from jax.sharding import PartitionSpec as P

HD = 64
ROT = 16
SEQ = 512
EPS = 1e-05
VMEM = 60 * 1024 * 1024
F32 = jnp.float32
BF16 = jnp.bfloat16


def dot(left, right, left_dim, right_dim):
    return lax.dot_general(
        left, right, (((left_dim,), (right_dim,)), ((), ())), preferred_element_type=F32
    )


def normalise(values):
    average = jnp.mean(values, axis=-1, keepdims=True)
    centred = values - average
    spread = jnp.mean(centred * centred, axis=-1, keepdims=True)
    scale = lax.rsqrt(spread + EPS)
    return centred * scale, scale


def norm_back(d, hat, scale, gain):
    dg = d * gain
    first = jnp.mean(dg, axis=-1, keepdims=True)
    second = jnp.mean(dg * hat, axis=-1, keepdims=True)
    return (dg - first - hat * second) * scale


def rotary_tables():
    half = ROT // 2
    rates = 10000.0 ** (-(2.0 * np.arange(half)) / ROT)
    angles = rates[:, None] * np.arange(SEQ)[None, :]
    return np.cos(angles).astype(np.float32), np.sin(angles).astype(np.float32)


def rotate(values, cosine, sine):
    half = ROT // 2
    first, second = values[:half], values[half:ROT]
    return jnp.concatenate(
        [first * cosine - second * sine, second * cosine + first * sine, values[ROT:]], axis=0
    )


def piece_rows(place, index, pieces, chunk):
    if pieces == 1:
        return pl.ds(0, chunk)
    across, core = index // 2, index % 2
    owner = (across ^ place[3]) * 2 + (core ^ place[4])
    return pl.ds(pl.multiple_of(owner * chunk, 16), chunk)


def assemble(place, refs, target):
    chunk = refs[0].shape[1]
    for index, ref in enumerate(refs):
        target[piece_rows(place, index, len(refs), chunk), :] = ref[0]


def share_out(place, source, held, made, pieces):
    for index in range(pieces):
        value = source[piece_rows(place, index, pieces, made[0].shape[1]), :]
        if held:
            value = value + held[index % 2][index // 2].astype(F32)
        made[index % 2][index // 2] = value.astype(BF16)


def prepare_kernel(place, *refs, part):
    *pieces, wt_ref, merge_ref, vec_ref, bias_ref, full = refs
    assemble(place, pieces, full)
    rows = wt_ref.shape[0]
    end = rows + merge_ref.shape[0]
    wt_ref[...] = full[:, :rows].T
    merge_ref[...] = full[:, rows:end].T
    vectors = full[:, end:].astype(F32)
    vec_ref[0] = vectors.T[: vec_ref.shape[1]]
    chunk = pieces[0].shape[1]
    if len(pieces) > 1:
        packed = [vectors[at : at + part] for at in range(0, vectors.shape[0], chunk)]
        bias_ref[0] = jnp.concatenate(packed, axis=0).T[: bias_ref.shape[1]]
    else:
        bias_ref[...] = jnp.zeros_like(bias_ref)


def attention_kernel(
    place, x_ref, g_ref, wt_ref, merge_ref, bias_ref, vec_ref, cos_ref, sin_ref, *refs,
    pieces, earlier,
):
    sides = min(pieces, 2)
    held, refs = refs[: sides * earlier], refs[sides * earlier :]
    out_ref, din_ref, rows_ref, hb_ref = refs[:4]
    made = refs[4 : 4 + sides]
    datt, att, dmix, acc = refs[4 + sides :]
    groups = wt_ref.shape[0] // (9 * HD)
    rows = 9 * HD
    half = SEQ // 2
    scaling = 1.0 / math.sqrt(HD)
    x = x_ref[...].astype(F32)
    g = g_ref[...]
    gain, shift = vec_ref[0, 4:5, :], vec_ref[0, 5:6, :]
    hat, scale = normalise(x)
    n1 = (hat * gain + shift).astype(BF16)
    datt[...] = dot(merge_ref[...], g, 1, 1).astype(BF16)
    cosine, sine = cos_ref[...], sin_ref[...]
    below = lax.broadcasted_iota(jnp.int32, (half, half), 0) <= lax.broadcasted_iota(
        jnp.int32, (half, half), 1
    )

    def raise_columns(scores):
        raised = jnp.exp(scores - jnp.max(scores, axis=0, keepdims=True))
        return raised, jnp.sum(raised, axis=0, keepdims=True)

    def group(index, carry):
        base = pl.multiple_of(index * rows, rows)
        part = dot(wt_ref[pl.ds(base, rows), :], n1, 1, 1)
        part = part + bias_ref[index].T[:, 0:1]
        for head in range(3):
            at = head * 3 * HD
            query = (rotate(part[at : at + HD], cosine, sine) * scaling).astype(BF16)
            keys = rotate(part[at + HD : at + 2 * HD], cosine, sine).astype(BF16)
            values = part[at + 2 * HD : at + 3 * HD].astype(BF16)
            spot = pl.multiple_of(index * 3 * HD + head * HD, HD)
            given = datt[pl.ds(spot, HD), :].astype(F32)
            keys_t, values_t = keys.T, values.T
            s0 = dot(keys_t[:half], query[:, :half], 1, 0)
            s1a = dot(keys_t[:half], query[:, half:], 1, 0)
            s1b = dot(keys_t[half:], query[:, half:], 1, 0)
            e0, l0 = raise_columns(jnp.where(below, s0, -1e30))
            e1, l1 = raise_columns(
                jnp.concatenate([s1a, jnp.where(below, s1b, -1e30)], axis=0)
            )
            w0, w1 = e0.astype(BF16), e1.astype(BF16)
            share = 1.0 / jnp.concatenate([l0, l1], axis=1)
            attended = share * jnp.concatenate(
                [dot(values[:, :half], w0, 1, 0), dot(values, w1, 1, 0)], axis=1
            )
            att[pl.ds(spot, HD), :] = attended.astype(BF16)
            given = (given * share).astype(BF16)
            level = jnp.sum(given.astype(F32) * attended, axis=0, keepdims=True)
            q0 = dot(values_t[:half], given[:, :half], 1, 0)
            q1 = dot(values_t, given[:, half:], 1, 0)
            d0 = (e0 * (q0 - level[:, :half])).astype(BF16)
            d1 = (e1 * (q1 - level[:, half:])).astype(BF16)
            d_values = dot(given[:, half:], w1, 1, 1)
            d_values = jnp.concatenate(
                [d_values[:, :half] + dot(given[:, :half], w0, 1, 1), d_values[:, half:]], axis=1
            )
            d_keys = dot(query[:, half:], d1, 1, 1)
            d_keys = jnp.concatenate(
                [d_keys[:, :half] + dot(query[:, :half], d0, 1, 1), d_keys[:, half:]], axis=1
            )
            d_query = jnp.concatenate(
                [dot(keys[:, :half], d0, 1, 0), dot(keys, d1, 1, 0)], axis=1
            ) * scaling
            to = pl.multiple_of(base + at, HD)
            dmix[pl.ds(to, HD), :] = rotate(d_query, cosine, -sine).astype(BF16)
            dmix[pl.ds(to + HD, HD), :] = rotate(d_keys, cosine, -sine).astype(BF16)
            dmix[pl.ds(to + 2 * HD, HD), :] = d_values.astype(BF16)
        return carry

    lax.fori_loop(0, groups, group, 0)
    out_ref[...] = dot(att[...].T, merge_ref[...], 1, 0).astype(BF16)
    d_first = dot(dmix[...].T, wt_ref[...], 1, 0)
    pair = place[1]
    mine = dmix[pl.ds(pl.multiple_of(pair * 2 * rows, 2 * rows), 2 * rows), :]
    mine_att = att[pl.ds(pl.multiple_of(pair * 6 * HD, 6 * HD), 6 * HD), :]
    hb_ref[0] = dot(jnp.ones((8, SEQ), BF16), mine, 1, 1)
    step = pl.program_id(0)

    @pl.when(step == 0)
    def _():
        acc[...] = jnp.zeros_like(acc)

    acc[:, : 2 * rows] += dot(n1.T, mine, 1, 1)
    acc[:, 2 * rows :] += dot(g.T, mine_att, 1, 1)

    @pl.when(step == pl.num_programs(0) - 1)
    def _():
        share_out(place, acc, held, made, pieces)

    rows_ref[0] = jnp.concatenate(
        [
            jnp.sum(d_first * hat, axis=0, keepdims=True),
            jnp.sum(d_first, axis=0, keepdims=True),
            jnp.sum(g.astype(F32), axis=0, keepdims=True),
            jnp.zeros((5, x.shape[1]), F32),
        ],
        axis=0,
    )
    din_ref[...] = norm_back(d_first, hat, scale, gain).astype(BF16)


def gelu_parts(h):
    near = 0.7071067811865476 * jnp.abs(h)
    below = 1.0 + 0.3275911 * near
    t = pl.reciprocal(below, approx=True)
    t = t * (2.0 - below * t)
    bell = jnp.exp(-0.5 * h * h)
    series = 1.061405429 * t - 1.453152027
    series = series * t + 1.421413741
    series = series * t - 0.284496736
    series = series * t + 0.254829592
    tail = 0.5 * series * t * bell
    phi = jnp.where(h >= 0, 1.0 - tail, tail)
    return h * phi, phi + h * bell * 0.3989422804014327


def feed_kernel(
    place, x_ref, g_ref, bias_ref, vec_ref, aout_ref, din_ref, *refs, pieces, earlier, at, phases,
):
    opens, closes = phases[0] == 0, phases[-1] == 1
    weights, refs = refs[:pieces], refs[pieces:]
    sides = min(pieces, 2)
    held, refs = refs[: sides * earlier], refs[sides * earlier :]
    begun, refs = refs[: 1 - opens], refs[1 - opens :]
    rows_ref, main_ref = refs[:2]
    made, refs = refs[2 : 2 + sides * opens], refs[2 + sides * opens :]
    n2, turned, n2t, gt, up, down, extra, part_s, acc, load_sem, held_sem, extra_sem, out_sem = refs
    chunk = weights[0].shape[1]
    ff = up.shape[2] // 2
    loads = {step: [] for step in phases}
    for step in phases:
        for index, ref in enumerate(weights):
            rows = piece_rows(place, index, pieces, chunk)
            for side in range(2):
                spot = slice(side * ff, (side + 1) * ff)
                for kind, target in enumerate((up, down)):
                    copy = pltpu.make_async_copy(
                        ref.at[2 * step + side, :, kind * ff : (kind + 1) * ff],
                        target.at[step, rows, spot],
                        load_sem.at[step, index, side, kind],
                    )
                    copy.start()
                    loads[step].append(copy)
    fetched = [
        pltpu.make_async_copy(held[k], part_s.at[k], held_sem.at[k])
        for k in range(sides * earlier)
    ]
    fetched += [
        pltpu.make_async_copy(ref.at[at * SEQ : (at + 1) * SEQ], extra.at[k], extra_sem.at[k])
        for k, ref in enumerate((aout_ref, din_ref))
    ]
    for copy in fetched:
        copy.start()

    gain, shift = vec_ref[0, 6:7, :], vec_ref[0, 7:8, :]
    hat, scale = normalise(x_ref[...].astype(F32))
    n2[...] = (hat * gain + shift).astype(BF16)
    if opens:
        for source, target in ((n2, n2t), (g_ref, gt)):
            turned[...] = source[...].T
            for index in range(pieces):
                rows = piece_rows(place, index, pieces, chunk)
                target[index * chunk : (index + 1) * chunk, :] = turned[rows, :]
    rows_ref[...] = jnp.zeros_like(rows_ref)
    stores = [pltpu.make_async_copy(part_s.at[k], made[k], out_sem.at[k]) for k in range(len(made))]

    def keep_gradients(activated, d_hidden):
        for copy in fetched[: sides * earlier]:
            copy.wait()
        for left, right, spot in ((n2t, d_hidden, 0), (gt, activated, 2 * ff)):
            fresh = dot(left[...], right, 1, 0)
            for index in range(pieces):
                value = fresh[index * chunk : (index + 1) * chunk, :]
                spots = (index % 2, index // 2, slice(None), slice(spot, spot + 2 * ff))
                if earlier:
                    value = value + part_s[spots].astype(F32)
                part_s[spots] = value.astype(BF16)
        for copy in stores:
            copy.start()
        sums = jnp.sum(d_hidden.astype(F32), axis=0, keepdims=True)
        rows_ref[2:3, :] = sums[:, :ff]
        rows_ref[3:4, :] = sums[:, ff:]

    def pair_of_groups(step, carry):
        for index, ref in enumerate(weights):
            for side in range(2):
                for kind, target in enumerate((up, down)):
                    pltpu.make_async_copy(
                        ref.at[side, :, :ff],
                        target.at[step, pl.ds(0, chunk), :ff],
                        load_sem.at[step, index, side, kind],
                    ).wait()
        which, parity = place[1] ^ step, place[2] % 2
        bias = jnp.concatenate(
            [bias_ref[2 * which + parity, 1:2, :], bias_ref[2 * which + 1 - parity, 1:2, :]],
            axis=1,
        )
        activated, slope = gelu_parts(dot(n2[...], up[step], 1, 0) + bias)
        activated = activated.astype(BF16)
        d_hidden = (dot(g_ref[...], down[step], 1, 0) * slope).astype(BF16)
        acc[0] += dot(activated, down[step], 1, 1)
        acc[1] += dot(d_hidden, up[step], 1, 1)
        if opens:
            pl.when(step == 0)(functools.partial(keep_gradients, activated, d_hidden))
        return carry

    acc[...] = begun[0][...] if begun else jnp.zeros_like(acc)
    lax.fori_loop(phases[0], phases[-1] + 1, pair_of_groups, 0)
    for copy in fetched[sides * earlier :]:
        copy.wait()
    if closes:
        d_second = acc[1]
        base = x_ref[...].astype(F32) + extra[0].astype(F32)
        base = base + vec_ref[0, 2:3, :] + vec_ref[0, 3:4, :]
        main_ref[0] = (acc[0] + base).astype(BF16)
        total = norm_back(d_second, hat, scale, gain) + extra[1].astype(F32)
        main_ref[1] = total.astype(BF16)
        rows_ref[0:1, :] = jnp.sum(d_second * hat, axis=0, keepdims=True)
        rows_ref[1:2, :] = jnp.sum(d_second, axis=0, keepdims=True)
    else:
        main_ref[...] = acc[...]
    for copy in stores:
        copy.wait()


def params(*kinds):
    return pltpu.CompilerParams(dimension_semantics=kinds, vmem_limit_bytes=VMEM)


def whole(shape):
    zeros = (0,) * len(shape)
    return pl.BlockSpec(shape, lambda *_: zeros)


def attention(place, x, g, wt, merge, bias, vecs, cosine, sine, count, pieces, earlier):
    width = x.shape[1]
    rows = 9 * HD
    columns = 2 * rows + 6 * HD
    given = pl.BlockSpec((SEQ, width), lambda i, place: (place[0] + i, 0))
    taken = pl.BlockSpec((SEQ, width), lambda i, place: (i, 0))

    def per(a, b):
        return pl.BlockSpec((1, a, b), lambda i, place: (i, 0, 0))

    sides = min(pieces, 2)
    part = (pieces // sides, width // pieces, columns)
    return pl.pallas_call(
        functools.partial(attention_kernel, pieces=pieces, earlier=1 if earlier else 0),
        grid_spec=pltpu.PrefetchScalarGridSpec(
            num_scalar_prefetch=1,
            grid=(count,),
            in_specs=[
                given, given, whole(wt.shape), whole(merge.shape), whole(bias.shape),
                whole((1, 8, width)), whole(cosine.shape), whole(sine.shape),
            ]
            + [whole(part)] * len(earlier),
            out_specs=[taken, taken, per(8, width), per(8, 2 * rows)]
            + [whole(part)] * sides,
            scratch_shapes=[
                pltpu.VMEM((width, SEQ), BF16),
                pltpu.VMEM((width, SEQ), BF16),
                pltpu.VMEM((wt.shape[0], SEQ), BF16),
                pltpu.VMEM((width, columns), F32),
            ],
        ),
        out_shape=[
            jax.ShapeDtypeStruct((count * SEQ, width), BF16),
            jax.ShapeDtypeStruct((count * SEQ, width), BF16),
            jax.ShapeDtypeStruct((count, 8, width), F32),
            jax.ShapeDtypeStruct((count, 8, 2 * rows), F32),
        ]
        + [jax.ShapeDtypeStruct(part, BF16)] * sides,
        compiler_params=params("arbitrary"),
        name="attention",
        cost_estimate=pl.CostEstimate(
            flops=count * 16_000_000_000, bytes_accessed=count * 12_000_000, transcendentals=0
        ),
    )(place, x, g, wt, merge, bias, vecs, cosine, sine, *earlier)


def feed(place, x, g, vecs, aout, din, at, weights, earlier, phases=(0, 1), begun=()):
    width = x.shape[1]
    groups, chunk, columns = weights[0].shape
    ff = columns // 2
    pieces = len(weights)
    sides = min(pieces, 2)
    given = pl.BlockSpec((SEQ, width), lambda s, place: (place[0], 0))
    part = (pieces // sides, chunk, 2 * columns)
    anywhere = pl.BlockSpec(memory_space=pl.ANY)
    first = 7 + pieces
    kept = 0 if begun else sides
    return pl.pallas_call(
        functools.partial(
            feed_kernel, pieces=pieces, earlier=1 if earlier else 0, at=at, phases=phases
        ),
        grid_spec=pltpu.PrefetchScalarGridSpec(
            num_scalar_prefetch=1,
            grid=(1,),
            in_specs=[given, given, whole(vecs.shape), whole((1, 8, width))]
            + [anywhere] * (2 + pieces + len(earlier))
            + [whole((2, SEQ, width))] * len(begun),
            out_specs=[whole((8, width)), whole((2, SEQ, width))] + [anywhere] * kept,
            scratch_shapes=[
                pltpu.VMEM((SEQ, width), BF16),
                pltpu.VMEM((width, SEQ), BF16),
                pltpu.VMEM((width, SEQ), BF16),
                pltpu.VMEM((width, SEQ), BF16),
                pltpu.VMEM((2, width, columns), BF16),
                pltpu.VMEM((2, width, columns), BF16),
                pltpu.VMEM((2, SEQ, width), BF16),
                pltpu.VMEM((sides, *part), BF16),
                pltpu.VMEM((2, SEQ, width), F32),
                pltpu.SemaphoreType.DMA((2, pieces, 2, 2)),
                pltpu.SemaphoreType.DMA((2,)),
                pltpu.SemaphoreType.DMA((2,)),
                pltpu.SemaphoreType.DMA((2,)),
            ],
        ),
        out_shape=[
            jax.ShapeDtypeStruct((8, width), F32),
            jax.ShapeDtypeStruct((2, SEQ, width), BF16 if phases[-1] == 1 else F32),
        ]
        + [jax.ShapeDtypeStruct(part, BF16)] * kept,
        input_output_aliases={first + k: 2 + k for k in range(len(earlier))},
        compiler_params=params("arbitrary"),
        name="feed",
        cost_estimate=pl.CostEstimate(
            flops=8_000_000_000 * len(phases), bytes_accessed=9_000_000, transcendentals=0
        ),
    )(place, x, g, vecs, vecs, aout, din, *weights, *earlier, *begun)


def prepare(place, weights, part):
    groups, chunk, columns = weights[0].shape
    pieces = len(weights)
    width = pieces * chunk
    rows = 9 * HD
    return pl.pallas_call(
        functools.partial(prepare_kernel, part=part),
        grid_spec=pltpu.PrefetchScalarGridSpec(
            num_scalar_prefetch=1,
            grid=(groups,),
            in_specs=[
                pl.BlockSpec((1, chunk, columns), lambda t, place: (t ^ place[2], 0, 0))
            ]
            * pieces,
            out_specs=[
                pl.BlockSpec((rows, width), lambda t, place: (t, 0)),
                pl.BlockSpec((3 * HD, width), lambda t, place: (t, 0)),
                pl.BlockSpec((1, 8, width), lambda t, place: (t, 0, 0)),
                pl.BlockSpec((1, 8, rows), lambda t, place: (t, 0, 0)),
            ],
            scratch_shapes=[pltpu.VMEM((width, columns), BF16)],
        ),
        out_shape=[
            jax.ShapeDtypeStruct((groups * rows, width), BF16),
            jax.ShapeDtypeStruct((groups * 3 * HD, width), BF16),
            jax.ShapeDtypeStruct((groups, 8, width), F32),
            jax.ShapeDtypeStruct((groups, 8, rows), F32),
        ],
        compiler_params=params("arbitrary"),
        name="prepare",
    )(place, *weights)


def trade(array, axis, mask):
    size = lax.axis_size(axis)
    return lax.ppermute(array, axis, [(i, i ^ mask) for i in range(size)])


def along(block):
    near, middle = trade(block, "tensor", 1), trade(block, "tensor", 2)
    return jnp.stack([block, near, middle, trade(tie(block, near), "tensor", 3)])


def across(block):
    return [block] + [trade(block, "dp", mask) for mask in (2, 4, 6)]


def both_cores(blocks):
    return [item for block in blocks for item in (block, trade(block, "dp", 1))]


def tie(array, after):
    return lax.optimization_barrier((array, after))[0]


def gather_both(early, late):
    own = early[None]
    others = [trade(early, "tensor", mask) for mask in (1, 2, 3)]
    own = across(own)
    others = jnp.stack(tie(others, own))
    late = along(tie(late, others))
    others = across(others)
    early = [jnp.concatenate(pair) for pair in zip(own, others)]
    ahead = late
    late = across(tie(late, early))
    early = both_cores([tie(item, ahead) for item in early])
    return early, late


def reduce_cores(kept, away):
    return kept.astype(F32) + trade(away, "dp", 1).astype(F32)


def exchange_across(pieces):
    return [pieces[0]] + [trade(pieces[k], "dp", 2 * k) for k in (1, 2, 3)]


def add_up(items):
    return sum(item.astype(F32) for item in items)


def body(
    block_input, cotangent, heads_weight, heads_bias, merge_weight, merge_bias, up_weight, up_bias,
    down_weight, down_bias, first_gain, first_shift, second_gain, second_shift,
):
    chunk = heads_weight.shape[0]
    owners = lax.axis_size("dp")
    groups = lax.axis_size("tensor")
    width = block_input.shape[1]
    spot = lax.axis_index("tensor")
    odd, pair = spot % 2, spot // 2
    total = block_input.shape[0] // SEQ
    count = total // 2
    fast = owners == 8 and groups == 4
    if fast:
        me = lax.axis_index("dp")
        facts = [odd * count, pair, spot, me // 2, me % 2]
    else:
        facts = [odd * count, pair, spot] + [jnp.zeros_like(spot)] * 2
    place = jnp.stack(facts).astype(jnp.int32)

    bias_part = heads_bias.shape[0]
    vectors = jnp.stack(
        [
            jnp.pad(heads_bias, (0, chunk - bias_part)), up_bias, merge_bias, down_bias,
            first_gain, first_shift, second_gain, second_shift,
        ],
        axis=1,
    )
    early = jnp.concatenate(
        [heads_weight, merge_weight.T, jnp.pad(vectors, ((0, 0), (0, 120)))], axis=1
    )
    late = jnp.concatenate([up_weight, down_weight.T], axis=1)
    if fast:
        early, late = gather_both(early, late)
    else:
        early, late = (
            lax.all_gather(item, ("tensor", "dp"), axis=0, tiled=True).reshape(groups, width, -1)
            for item in (early, late)
        )
        early, late = ([item[spot ^ jnp.arange(groups)]] for item in (early, late))
    rows = 9 * HD
    wt, merge, vecs, hbias = prepare(place, early, bias_part)
    if not fast:
        hbias = vecs[:, 0].reshape(groups, owners, chunk)[:, :, :bias_part]
        hbias = jnp.broadcast_to(hbias.reshape(groups, 1, rows), (groups, 8, rows))
    ff = up_weight.shape[1]
    cosine, sine = rotary_tables()
    swap = [(i, i ^ 1) for i in range(groups)]
    def shifted(i):
        return place.at[0].add(i)

    def attend(i, number, earlier, after):
        return attention(
            tie(shifted(i), after), block_input, cotangent, wt, merge, hbias, vecs, cosine, sine,
            number, len(early), earlier,
        )

    def advance(i, source, at, done, after):
        common = tie(shifted(i), after), block_input, cotangent, vecs, *source[:2], at, late
        sums, rows16, *grads = feed(*common, done[2:])
        return [rows16, sums, *grads], trade(rows16, "tensor", 1)

    lead = count - 1
    first = attend(0, lead, [], ())
    if fast:
        late = both_cores(tie(late, first[0]))
    second = attend(lead, 1, first[4:], late[0])
    done, others, totals = [], [], []
    wait = second[2]
    for i in range(count):
        source, at = (first, i) if i < lead else (second, 0)
        done, other = advance(i, source, at, done, wait)
        others.append((done[0], other))
        totals.append(done[1])
        if i == 0 and fast:
            heads_part = reduce_cores(*second[4:]).astype(BF16)
            wait = heads_part
        if i == 1:
            wait = others[0]
            if fast:
                heads_items = exchange_across(heads_part)
                wait = wait, heads_items
    if fast:
        heads_cols = add_up(tie(heads_items, done[1])).astype(BF16)
    else:
        heads_cols = lax.psum_scatter(second[4][0], "dp", scatter_dimension=0, tiled=True)

    rows_a = first[2].sum(0) + second[2].sum(0)
    hb = (first[3].sum(0) + second[3].sum(0))[0]
    rows_f = sum(totals)
    hb = jnp.pad(hb.reshape(2, owners, bias_part), ((0, 0), (0, 0), (0, chunk - bias_part)))
    small = jnp.concatenate(
        [
            rows_a[0:2], rows_f[0:2], rows_a[2:3], rows_f[2:4], hb.reshape(2, width),
            jnp.zeros((3, width), F32),
        ],
        axis=0,
    )
    if fast:
        kept, away = done[2:]
        kept = reduce_cores(kept, away).astype(BF16)
        small = (small + trade(small, "dp", 1)).reshape(-1, 4 * ff)
        tail = small.shape[0]
        small = jnp.pad(small, ((0, 8 - tail), (0, 0))).astype(BF16)
        kept = tie(kept, others[-2][1])
        ready = kept
        feed_cols = add_up(exchange_across([jnp.concatenate([item, small]) for item in kept]))
        small = feed_cols[chunk : chunk + tail].reshape(-1, width)
        small = lax.dynamic_slice(small, (0, me * chunk), (small.shape[0], chunk))
        feed_cols = feed_cols[:chunk].astype(BF16)
    else:
        ready = done[1]
        feed_cols = lax.psum_scatter(done[2][0], "dp", scatter_dimension=0, tiled=True)
        small = lax.psum_scatter(small, "dp", scatter_dimension=1, tiled=True)

    def settle(mine, other):
        return mine.astype(F32) + trade(other, "tensor", 1).astype(F32)

    small = small + trade(
        jnp.concatenate([small[:5], small[6:7], small[5:6], small[7:]], axis=0), "tensor", 1
    )
    feed_sum = settle(
        *(
            jnp.concatenate([feed_cols[:, k : k + ff], feed_cols[:, k + 2 * ff : k + 3 * ff]], axis=1)
            for k in (0, ff)
        )
    )
    wide = 2 * rows
    heads_cols = jnp.concatenate(
        [
            heads_cols[:, :rows], heads_cols[:, wide : wide + 3 * HD],
            heads_cols[:, rows:wide], heads_cols[:, wide + 3 * HD :],
        ],
        axis=1,
    )
    heads_cols = tie(heads_cols, ready)
    others[-1] = others[-1][0], tie(others[-1][1], ready)
    half = rows + 3 * HD
    left, right = heads_cols[:, :half], heads_cols[:, half:]
    heads_sum = settle(jnp.where(odd == 0, left, right), jnp.where(odd == 0, right, left))

    layer_output = tie(jnp.zeros(block_input.shape, BF16), done[1])
    input_grad = tie(jnp.zeros(block_input.shape, F32), ready)
    for i, both in enumerate(others):
        for item, base in zip(both, (odd, 1 - odd)):
            at = (base * count + i) * SEQ
            layer_output = lax.dynamic_update_slice(layer_output, item[0], (at, 0))
            given = lax.dynamic_slice(cotangent, (at, 0), (SEQ, width))
            input_grad = lax.dynamic_update_slice(
                input_grad, item[1].astype(F32) + given.astype(F32), (at, 0)
            )
    return (
        layer_output,
        input_grad,
        heads_sum[:, :rows],
        jnp.where(odd == 0, small[7], small[8])[:bias_part],
        heads_sum[:, rows:].T,
        small[4],
        feed_sum[:, :ff],
        small[5],
        feed_sum[:, ff:].T,
        small[4],
        small[0],
        small[1],
        small[2],
        small[3],
    )


def solution(mesh):
    placed = (
        P("dp", None),
        P("dp", None),
        P("dp", "tensor"),
        P(("tensor", "dp")),
        P("tensor", "dp"),
        P("dp"),
        P("dp", "tensor"),
        P(("tensor", "dp")),
        P("tensor", "dp"),
        P("dp"),
        P("dp"),
        P("dp"),
        P("dp"),
        P("dp"),
    )
    return jax.shard_map(
        body,
        mesh=mesh,
        in_specs=placed,
        out_specs=placed,
        check_vma=False,
    )
```

profile of v0, /device:TPU:0, one launch (start us, length us, event | category | flops | bytes accessed | tf_op | source)
XLA Modules:
  0.0 289.6 jit_solution(1960407548221676126)
XLA Ops:
  0.7 0.9 copy.44
  2.3 0.8 stack.86
  3.2 1.0 fusion.22
  4.2 3.0 %collective-permute-start.3 = (bf16[1,96,896]{2,1,0:T(8,128)(2,1)S(1)}, bf16[1,96,896]{2,1,0:T(8,128)(2,1)S(1)}, u32[]{:S(2)}, u32[]{:S(2)}) collective-permute-start(bf16[1,96,896]{2,1,0:T(8,128)(2,1)S(1)} %fusion.22), channel_id=1, source_target_pairs={{0,8},{4,12},{8,0},{12,4},{16,24},{20,28},{24,16},{28,20},{1,9},{5... | collective-permute-start | bytes 516104 | tf_op jit(solution)/shard_map/ppermute | solution.py:470
  7.2 1.5 collective-permute-start.4
  8.7 1.0 fusion.14
  9.7 2.1 collective-permute-start
  11.8 2.6 collective-permute-start.1
  14.4 2.1 collective-permute-start.2
  16.7 0.7 collective-permute-done
  17.4 9.5 %collective-permute-done.1 = bf16[96,896]{1,0:T(8,128)(2,1)S(1)} collective-permute-done((bf16[96,896]{1,0:T(8,128)(2,1)S(1)}, bf16[96,896]{1,0:T(8,128)(2,1)S(1)}, u32[]{:S(2)}, u32[]{:S(2)}) %collective-permute-start.1) | collective-permute-done | bytes 172064 | tf_op jit(solution)/shard_map/ppermute | solution.py:470
  27.0 2.5 collective-permute-start.11
  29.6 2.5 collective-permute-start.6
  32.0 1.1 collective-permute-start.7
  35.0 7.5 %collective-permute-done.6 = bf16[96,1536]{1,0:T(8,128)(2,1)S(1)} collective-permute-done((bf16[96,1536]{1,0:T(8,128)(2,1)S(1)}, bf16[96,1536]{1,0:T(8,128)(2,1)S(1)}, u32[]{:S(2)}, u32[]{:S(2)}) %collective-permute-start.6) | collective-permute-done | bytes 294944 | tf_op jit(solution)/shard_map/ppermute | solution.py:470
  42.6 1.6 collective-permute-start.8
  44.2 0.8 constant_dynamic-update-slice_fusion.4.refs_6_
  45.0 3.4 %collective-permute-done.10 = bf16[3,96,896]{2,1,0:T(8,128)(2,1)S(1)} collective-permute-done((bf16[3,96,896]{2,1,0:T(8,128)(2,1)S(1)}, bf16[3,96,896]{2,1,0:T(8,128)(2,1)S(1)}, u32[]{:S(2)}, u32[]{:S(2)}) %collective-permute-start.10) | collective-permute-done | bytes 516128 | tf_op jit(solution)/shard_map/ppermute | solution.py:470
  48.6 5.0 %collective-permute-done.7 = bf16[96,1536]{1,0:T(8,128)(2,1)S(1)} collective-permute-done((bf16[96,1536]{1,0:T(8,128)(2,1)S(1)}, bf16[96,1536]{1,0:T(8,128)(2,1)S(1)}, u32[]{:S(2)}, u32[]{:S(2)}) %collective-permute-start.7) | collective-permute-done | bytes 294944 | tf_op jit(solution)/shard_map/ppermute | solution.py:470
  57.1 1.5 collective-permute-start.14
  59.1 7.4 %prepare.1 = (bf16[2304,768]{1,0:T(8,128)(2,1)}, bf16[768,768]{1,0:T(8,128)(2,1)}, f32[4,8,768]{2,1,0:T(8,128)}, f32[4,8,576]{2,1,0:T(8,128)}) custom-call(s32[5]{0:T(128)} %copy-done.22, bf16[4,96,896]{2,1,0:T(8,128)(2,1)} %copy-done, bf16[4,96,896]{2,1,0:T(8,128)(2,1)} %collective-permute-done.15.refs_1_, bf16[4,96,896]{2,1,0:T(8,128)(2,1)} %copy-done.12, ...), custom_call_target="tpu_custom_call" | custom-call | tf_op jit(solution)/shard_map/prepare/pallas_call | solution.py:440
  66.5 43.1 %attention.2 = (bf16[1024,768]{1,0:T(8,128)(2,1)}, bf16[1024,768]{1,0:T(8,128)(2,1)}, f32[2,8,768]{2,1,0:T(8,128)}, f32[2,8,1152]{2,1,0:T(8,128)}, bf16[4,96,153...) custom-call(s32[5]{0:T(128)} %copy-done.27, bf16[3072,768]{1,0:T(8,128)(2,1)} %x_ref.9, bf16[3072,768]{1,0:T(8,128)(2,1)} %g_ref.9, ...), custom_call_target="tpu_custom_call" | custom-call | flops 32000000000 | bytes 24000000 | tf_op jit(solution)/shard_map/attention/pallas_call | solution.py:349
  109.6 0.9 reduce_sum.32
  110.5 0.8 reduce_sum.23
  112.4 23.6 %attention.3 = (bf16[512,768]{1,0:T(8,128)(2,1)}, bf16[512,768]{1,0:T(8,128)(2,1)}, f32[1,8,768]{2,1,0:T(8,128)}, f32[1,8,1152]{2,1,0:T(8,128)}, bf16[4,96,1536]...) custom-call(s32[5]{0:T(128)} %copy-done.24, bf16[3072,768]{1,0:T(8,128)(2,1)} %x_ref.9, bf16[3072,768]{1,0:T(8,128)(2,1)} %g_ref.9, ...), custom_call_target="tpu_custom_call" | custom-call | flops 16000000000 | bytes 12000000 | tf_op jit(solution)/shard_map/attention/pallas_call | solution.py:349
  136.1 0.7 bitcast_add_fusion
  137.0 0.8 fusion.15
  138.0 23.5 %feed.3 = (f32[8,768]{1,0:T(8,128)}, bf16[2,512,768]{2,1,0:T(8,128)(2,1)}, bf16[4,96,3072]{2,1,0:T(8,128)(2,1)}, bf16[4,96,3072]{2,1,0:T(8,128)(2,1)}) custom-call(s32[5]{0:T(128)} %copy-done.27, bf16[3072,768]{1,0:T(8,128)(2,1)} %x_ref.9, bf16[3072,768]{1,0:T(8,128)(2,1)} %g_ref.9, f32[4,8,768]{2,1,0:T(8,128)} %get-tuple-element.134.vec_ref.bias_ref, ...), custom_call_target="tpu_custom_call" | custom-call | flops 16000000000 | bytes 9000000 | tf_op jit(solution)/shard_map/feed/pallas_call | solution.py:394
  161.5 5.7 %collective-permute-start.23 = (bf16[2,512,768]{2,1,0:T(8,128)(2,1)}, bf16[2,512,768]{2,1,0:T(8,128)(2,1)S(1)}, u32[]{:S(2)}, u32[]{:S(2)}) collective-permute-start(bf16[2,512,768]{2,1,0:T(8,128)(2,1)} %get-tuple-element.146), channel_id=1, source_target_pairs={{0,1},{1,0},{2,3},{3,2},{4,5},{5,4},{6,7},{7,6},{8,9},{9,8},{10,11... | collective-permute-start | bytes 4718600 | tf_op jit(solution)/shard_map/ppermute | solution.py:470
  167.6 0.8 collective-permute-start.25
  169.2 2.0 collective-permute-start.27
  171.2 23.3 %feed.4 = (f32[8,768]{1,0:T(8,128)}, bf16[2,512,768]{2,1,0:T(8,128)(2,1)}, bf16[4,96,3072]{2,1,0:T(8,128)(2,1)}, bf16[4,96,3072]{2,1,0:T(8,128)(2,1)}) custom-call(s32[5]{0:T(128)} %copy-done.26, bf16[3072,768]{1,0:T(8,128)(2,1)} %x_ref.9, bf16[3072,768]{1,0:T(8,128)(2,1)} %g_ref.9, ...), custom_call_target="tpu_custom_call", output_to_operand_aliasing={{2}: (15, {}), {3}: (16, {})} | custom-call | flops 16000000000 | bytes 9000000 | tf_op jit(solution)/shard_map/feed/pallas_call | solution.py:394
  194.6 8.1 %collective-permute-done.23 = bf16[2,512,768]{2,1,0:T(8,128)(2,1)S(1)} collective-permute-done((bf16[2,512,768]{2,1,0:T(8,128)(2,1)}, bf16[2,512,768]{2,1,0:T(8,128)(2,1)S(1)}, u32[]{:S(2)}, u32[]{:S(2)}) %collective-permute-start.23) | collective-permute-done | bytes 1572896 | tf_op jit(solution)/shard_map/ppermute | solution.py:470
  202.7 23.4 %feed.5 = (f32[8,768]{1,0:T(8,128)}, bf16[2,512,768]{2,1,0:T(8,128)(2,1)}, bf16[4,96,3072]{2,1,0:T(8,128)(2,1)}, bf16[4,96,3072]{2,1,0:T(8,128)(2,1)}) custom-call(s32[5]{0:T(128)} %copy-done.24, bf16[3072,768]{1,0:T(8,128)(2,1)} %x_ref.9, bf16[3072,768]{1,0:T(8,128)(2,1)} %g_ref.9, ...), custom_call_target="tpu_custom_call", output_to_operand_aliasing={{2}: (15, {}), {3}: (16, {})} | custom-call | flops 16000000000 | bytes 9000000 | tf_op jit(solution)/shard_map/feed/pallas_call | solution.py:394
  226.2 0.7 add_add_fusion
  228.0 2.0 collective-permute-start.29
  230.0 1.3 add_convert_fusion.2
  231.4 2.5 broadcast_in_dim.12
  233.9 0.9 bitcast_dynamic-update-slice_fusion.3
  234.8 0.8 copy-done.4
  235.6 0.9 fusion.8
  236.5 0.9 bitcast_dynamic-update-slice_fusion.2
  237.4 2.1 fusion.7
  239.5 0.9 bitcast_dynamic-update-slice_fusion.1
  240.7 2.6 add_convert_fusion
  243.4 1.0 fusion.10
  244.4 0.8 collective-permute-start.33
  245.9 2.0 collective-permute-start.35
  248.0 1.1 collective-permute-start.31
  249.1 4.3 %broadcast_in_dim.14 = f32[3072,768]{1,0:T(8,128)} broadcast(f32[]{:T(128)} %constant.156.clone.1), dimensions={} | broadcast | bytes 9437188 | tf_op jit(solution)/shard_map/broadcast_in_dim | solution.py:658
  253.5 1.3 fusion.5
  255.4 1.3 fusion.4
  257.4 1.3 fusion.3
  258.7 2.6 fusion.2
  261.3 1.3 fusion.1
  262.6 7.6 %collective-permute-done.29 = bf16[2,512,768]{2,1,0:T(8,128)(2,1)} collective-permute-done((bf16[2,512,768]{2,1,0:T(8,128)(2,1)}, bf16[2,512,768]{2,1,0:T(8,128)(2,1)}, u32[]{:S(2)}, u32[]{:S(2)}) %collective-permute-start.29) | collective-permute-done | bytes 1572896 | tf_op jit(solution)/shard_map/ppermute | solution.py:470
  270.2 2.4 fusion
  272.6 2.1 bitcast_dynamic-update-slice_fusion
  275.6 0.7 copy.46
  276.3 1.5 fusion.16
  278.1 2.0 collective-permute-start.36
  280.3 1.6 collective-permute-done.36
  283.0 4.9 %collective-permute-done.37 = bf16[96,1536]{1,0:T(8,128)(2,1)S(1)} collective-permute-done((bf16[96,1536]{1,0:T(8,128)(2,1)S(1)}, bf16[96,1536]{1,0:T(8,128)(2,1)S(1)}, u32[]{:S(2)}, u32[]{:S(2)}) %collective-permute-start.37) | collective-permute-done | bytes 294944 | tf_op jit(solution)/shard_map/ppermute | solution.py:470
  288.0 0.9 slice_bitcast_fusion.8
  (159 shorter events, 16.1 us)
Async XLA Ops:
  0.6 28.9 %copy-start.17 = (bf16[768,96]{0,1:T(8,128)(2,1)S(1)}, bf16[768,96]{0,1:T(8,128)(2,1)}, u32[]{:S(2)}) copy-start(bf16[768,96]{0,1:T(8,128)(2,1)} %param.34) | copy-start | bytes 442372
  0.7 28.9 %copy-start.18 = (bf16[96,768]{1,0:T(8,128)(2,1)S(1)}, bf16[96,768]{1,0:T(8,128)(2,1)}, u32[]{:S(2)}) copy-start(bf16[96,768]{1,0:T(8,128)(2,1)} %param.32) | copy-start | bytes 442372
  4.2 10.2 %collective-permute-start.3 = (bf16[1,96,896]{2,1,0:T(8,128)(2,1)S(1)}, bf16[1,96,896]{2,1,0:T(8,128)(2,1)S(1)}, u32[]{:S(2)}, u32[]{:S(2)}) collective-permute-start(bf16[1,96,896]{2,1,0:T(8,128)(2,1)S(1)} %fusion.22), channel_id=1, source_target_pairs={{0,8},{4,12},{8,0},{12,4},{16,24},{20,28},{24,16},{28,20},{1,9},{5... | collective-permute-start | bytes 516104 | tf_op jit(solution)/shard_map/ppermute | solution.py:470
  7.2 9.5 %collective-permute-start.4 = (bf16[1,96,896]{2,1,0:T(8,128)(2,1)S(1)}, bf16[1,96,896]{2,1,0:T(8,128)(2,1)S(1)}, u32[]{:S(2)}, u32[]{:S(2)}) collective-permute-start(bf16[1,96,896]{2,1,0:T(8,128)(2,1)S(1)} %fusion.22), channel_id=1, source_target_pairs={{0,16},{4,20},{8,24},{12,28},{16,0},{20,4},{24,8},{28,12},{1,17},{... | collective-permute-start | bytes 516104 | tf_op jit(solution)/shard_map/ppermute | solution.py:470
  8.7 8.0 %collective-permute-start.5 = (bf16[1,96,896]{2,1,0:T(8,128)(2,1)S(1)}, bf16[1,96,896]{2,1,0:T(8,128)(2,1)S(1)}, u32[]{:S(2)}, u32[]{:S(2)}) collective-permute-start(bf16[1,96,896]{2,1,0:T(8,128)(2,1)S(1)} %fusion.22), channel_id=1, source_target_pairs={{0,24},{4,28},{8,16},{12,20},{16,8},{20,12},{24,0},{28,4},{1,25},{... | collective-permute-start | bytes 516104 | tf_op jit(solution)/shard_map/ppermute | solution.py:470
  9.7 7.7 %collective-permute-start = (bf16[96,896]{1,0:T(8,128)(2,1)S(1)}, bf16[96,896]{1,0:T(8,128)(2,1)S(1)}, u32[]{:S(2)}, u32[]{:S(2)}) collective-permute-start(bf16[96,896]{1,0:T(8,128)(2,1)S(1)} %fusion.14), channel_id=1, source_target_pairs={{0,1},{1,0},{2,3},{3,2},{4,5},{5,4},{6,7},{7,6},{8,9},{9,8},{10,11... | collective-permute-start | bytes 516104 | tf_op jit(solution)/shard_map/ppermute | solution.py:470
  11.8 15.2 %collective-permute-start.1 = (bf16[96,896]{1,0:T(8,128)(2,1)S(1)}, bf16[96,896]{1,0:T(8,128)(2,1)S(1)}, u32[]{:S(2)}, u32[]{:S(2)}) collective-permute-start(bf16[96,896]{1,0:T(8,128)(2,1)S(1)} %fusion.14), channel_id=1, source_target_pairs={{0,2},{1,3},{2,0},{3,1},{4,6},{5,7},{6,4},{7,5},{8,10},{9,11},{10,... | collective-permute-start | bytes 516104 | tf_op jit(solution)/shard_map/ppermute | solution.py:470
  14.4 12.6 %collective-permute-start.2 = (bf16[96,896]{1,0:T(8,128)(2,1)S(1)}, bf16[96,896]{1,0:T(8,128)(2,1)S(1)}, u32[]{:S(2)}, u32[]{:S(2)}) collective-permute-start(bf16[96,896]{1,0:T(8,128)(2,1)S(1)} %fusion.14), channel_id=1, source_target_pairs={{0,3},{1,2},{2,1},{3,0},{4,7},{5,6},{6,5},{7,4},{8,11},{9,10},{10,... | collective-permute-start | bytes 516104 | tf_op jit(solution)/shard_map/ppermute | solution.py:470
  27.0 17.2 %collective-permute-start.11 = (bf16[3,96,896]{2,1,0:T(8,128)(2,1)S(1)}, bf16[3,96,896]{2,1,0:T(8,128)(2,1)S(1)}, u32[]{:S(2)}, u32[]{:S(2)}) collective-permute-start(bf16[3,96,896]{2,1,0:T(8,128)(2,1)S(1)} %pad_maximum_fusion.2), channel_id=1, source_target_pairs={{0,24},{4,28},{8,16},{12,20},{16,8},{20,12},{24,0},{28,4},{1,25},{... | collective-permute-start | bytes 1548296 | tf_op jit(solution)/shard_map/ppermute | solution.py:470
  29.6 13.0 %collective-permute-start.6 = (bf16[96,1536]{1,0:T(8,128)(2,1)S(1)}, bf16[96,1536]{1,0:T(8,128)(2,1)S(1)}, u32[]{:S(2)}, u32[]{:S(2)}) collective-permute-start(bf16[96,1536]{1,0:T(8,128)(2,1)S(1)} %pad_maximum_fusion.3), channel_id=1, source_target_pairs={{0,1},{1,0},{2,3},{3,2},{4,5},{5,4},{6,7},{7,6},{8,9},{9,8},{10,11... | collective-permute-start | bytes 884744 | tf_op jit(solution)/shard_map/ppermute | solution.py:470
  32.0 21.5 %collective-permute-start.7 = (bf16[96,1536]{1,0:T(8,128)(2,1)S(1)}, bf16[96,1536]{1,0:T(8,128)(2,1)S(1)}, u32[]{:S(2)}, u32[]{:S(2)}) collective-permute-start(bf16[96,1536]{1,0:T(8,128)(2,1)S(1)} %pad_maximum_fusion.3), channel_id=1, source_target_pairs={{0,2},{1,3},{2,0},{3,1},{4,6},{5,7},{6,4},{7,5},{8,10},{9,11},{10,... | collective-permute-start | bytes 884744 | tf_op jit(solution)/shard_map/ppermute | solution.py:470
  33.1 15.3 %collective-permute-start.10 = (bf16[3,96,896]{2,1,0:T(8,128)(2,1)S(1)}, bf16[3,96,896]{2,1,0:T(8,128)(2,1)S(1)}, u32[]{:S(2)}, u32[]{:S(2)}) collective-permute-start(bf16[3,96,896]{2,1,0:T(8,128)(2,1)S(1)} %pad_maximum_fusion.2), channel_id=1, source_target_pairs={{0,16},{4,20},{8,24},{12,28},{16,0},{20,4},{24,8},{28,12},{1,17},{... | collective-permute-start | bytes 1548296 | tf_op jit(solution)/shard_map/ppermute | solution.py:470
  33.6 14.9 %collective-permute-start.9 = (bf16[3,96,896]{2,1,0:T(8,128)(2,1)S(1)}, bf16[3,96,896]{2,1,0:T(8,128)(2,1)S(1)}, u32[]{:S(2)}, u32[]{:S(2)}) collective-permute-start(bf16[3,96,896]{2,1,0:T(8,128)(2,1)S(1)} %pad_maximum_fusion.2), channel_id=1, source_target_pairs={{0,8},{4,12},{8,0},{12,4},{16,24},{20,28},{24,16},{28,20},{1,9},{5... | collective-permute-start | bytes 1548296 | tf_op jit(solution)/shard_map/ppermute | solution.py:470
  35.0 19.4 %copy-start = (bf16[4,96,896]{2,1,0:T(8,128)(2,1)}, bf16[4,96,896]{2,1,0:T(8,128)(2,1)S(1)}, u32[]{:S(2)}) copy-start(bf16[4,96,896]{2,1,0:T(8,128)(2,1)S(1)} %pad_maximum_fusion.1.refs_0_) | copy-start | bytes 2064388
  42.6 11.0 %collective-permute-start.8 = (bf16[96,1536]{1,0:T(8,128)(2,1)S(1)}, bf16[96,1536]{1,0:T(8,128)(2,1)S(1)}, u32[]{:S(2)}, u32[]{:S(2)}) collective-permute-start(bf16[96,1536]{1,0:T(8,128)(2,1)S(1)} %pad_maximum_fusion.3), channel_id=1, source_target_pairs={{0,3},{1,2},{2,1},{3,0},{4,7},{5,6},{6,5},{7,4},{8,11},{9,10},{10,... | collective-permute-start | bytes 884744 | tf_op jit(solution)/shard_map/ppermute | solution.py:470
  48.5 5.3 %copy-start.13 = (bf16[4,96,896]{2,1,0:T(8,128)(2,1)}, bf16[4,96,896]{2,1,0:T(8,128)(2,1)S(1)}, u32[]{:S(2)}) copy-start(bf16[4,96,896]{2,1,0:T(8,128)(2,1)S(1)} %constant_dynamic-update-slice_fusion.2.refs_4_) | copy-start | bytes 2064388
  48.6 10.5 %copy-start.12 = (bf16[4,96,896]{2,1,0:T(8,128)(2,1)}, bf16[4,96,896]{2,1,0:T(8,128)(2,1)S(1)}, u32[]{:S(2)}) copy-start(bf16[4,96,896]{2,1,0:T(8,128)(2,1)S(1)} %constant_dynamic-update-slice_fusion.refs_2_) | copy-start | bytes 2064388
  53.7 57.6 %copy-start.11 = (bf16[4,96,1536]{2,1,0:T(8,128)(2,1)}, bf16[4,96,1536]{2,1,0:T(8,128)(2,1)S(1)}, u32[]{:S(2)}) copy-start(bf16[4,96,1536]{2,1,0:T(8,128)(2,1)S(1)} %pad_maximum_fusion.refs_0_) | copy-start | bytes 3538948
  53.8 2.6 collective-permute-start.18
  53.8 3.2 %collective-permute-start.17 = (bf16[4,96,896]{2,1,0:T(8,128)(2,1)S(1)}, bf16[4,96,896]{2,1,0:T(8,128)(2,1)}, u32[]{:S(2)}, u32[]{:S(2)}) collective-permute-start(bf16[4,96,896]{2,1,0:T(8,128)(2,1)S(1)} %constant_dynamic-update-slice_fusion.2.refs_4_), channel_id=1, source_target_pairs={{0,4},{4,0},{8,12},{12,8},{16,20},{20,16},{24,28},{28,24},{1,5},{5... | collective-permute-start | bytes 2064392 | tf_op jit(solution)/shard_map/ppermute | solution.py:470
  54.3 4.3 %collective-permute-start.16 = (bf16[4,96,896]{2,1,0:T(8,128)(2,1)S(1)}, bf16[4,96,896]{2,1,0:T(8,128)(2,1)}, u32[]{:S(2)}, u32[]{:S(2)}) collective-permute-start(bf16[4,96,896]{2,1,0:T(8,128)(2,1)S(1)} %constant_dynamic-update-slice_fusion.refs_2_), channel_id=1, source_target_pairs={{0,4},{4,0},{8,12},{12,8},{16,20},{20,16},{24,28},{28,24},{1,5},{5... | collective-permute-start | bytes 2064392 | tf_op jit(solution)/shard_map/ppermute | solution.py:470
  54.4 4.6 %collective-permute-start.15 = (bf16[4,96,896]{2,1,0:T(8,128)(2,1)S(1)}, bf16[4,96,896]{2,1,0:T(8,128)(2,1)}, u32[]{:S(2)}, u32[]{:S(2)}) collective-permute-start(bf16[4,96,896]{2,1,0:T(8,128)(2,1)S(1)} %pad_maximum_fusion.1.refs_0_), channel_id=1, source_target_pairs={{0,4},{4,0},{8,12},{12,8},{16,20},{20,16},{24,28},{28,24},{1,5},{5... | collective-permute-start | bytes 2064392 | tf_op jit(solution)/shard_map/ppermute | solution.py:470
  54.9 4.1 %copy-start.22 = (s32[5]{0:T(128)}, s32[5]{0:T(128)S(1)}, u32[]{:S(2)}) copy-start(s32[5]{0:T(128)S(1)} %stack.77.place) | copy-start | bytes 64
  55.0 11.5 %copy-start.27 = (s32[5]{0:T(128)}, s32[5]{0:T(128)S(1)}, u32[]{:S(2)}) copy-start(s32[5]{0:T(128)S(1)} %constant_dynamic-update-slice_fusion.7.place) | copy-start | bytes 64
  55.0 11.5 %copy-start.26 = (s32[5]{0:T(128)}, s32[5]{0:T(128)S(1)}, u32[]{:S(2)}) copy-start(s32[5]{0:T(128)S(1)} %constant_dynamic-update-slice_fusion.6.place) | copy-start | bytes 64
  55.1 56.3 %collective-permute-start.12 = (bf16[4,96,1536]{2,1,0:T(8,128)(2,1)S(1)}, bf16[4,96,1536]{2,1,0:T(8,128)(2,1)}, u32[]{:S(2)}, u32[]{:S(2)}) collective-permute-start(bf16[4,96,1536]{2,1,0:T(8,128)(2,1)S(1)} %pad_maximum_fusion.refs_0_), channel_id=1, source_target_pairs={{0,8},{4,12},{8,0},{12,4},{16,24},{20,28},{24,16},{28,20},{1,9},{5... | collective-permute-start | bytes 3538952 | tf_op jit(solution)/shard_map/ppermute | solution.py:470
  56.4 54.9 %collective-permute-start.13 = (bf16[4,96,1536]{2,1,0:T(8,128)(2,1)S(1)}, bf16[4,96,1536]{2,1,0:T(8,128)(2,1)}, u32[]{:S(2)}, u32[]{:S(2)}) collective-permute-start(bf16[4,96,1536]{2,1,0:T(8,128)(2,1)S(1)} %pad_maximum_fusion.refs_0_), channel_id=1, source_target_pairs={{0,16},{4,20},{8,24},{12,28},{16,0},{20,4},{24,8},{28,12},{1,17},{... | collective-permute-start | bytes 3538952 | tf_op jit(solution)/shard_map/ppermute | solution.py:470
  57.1 54.3 %collective-permute-start.14 = (bf16[4,96,1536]{2,1,0:T(8,128)(2,1)S(1)}, bf16[4,96,1536]{2,1,0:T(8,128)(2,1)}, u32[]{:S(2)}, u32[]{:S(2)}) collective-permute-start(bf16[4,96,1536]{2,1,0:T(8,128)(2,1)S(1)} %pad_maximum_fusion.refs_0_), channel_id=1, source_target_pairs={{0,24},{4,28},{8,16},{12,20},{16,8},{20,12},{24,0},{28,4},{1,25},{... | collective-permute-start | bytes 3538952 | tf_op jit(solution)/shard_map/ppermute | solution.py:470
  66.5 43.1 %copy-start.23 = (s32[5]{0:T(128)S(1)}, s32[5]{0:T(128)}, u32[]{:S(2)}) copy-start(s32[5]{0:T(128)} %copy-done.22) | copy-start | bytes 64
  109.6 2.8 copy-start.24
  111.3 26.6 %collective-permute-start.19 = (bf16[4,96,1536]{2,1,0:T(8,128)(2,1)S(1)}, bf16[4,96,1536]{2,1,0:T(8,128)(2,1)}, u32[]{:S(2)}, u32[]{:S(2)}) collective-permute-start(bf16[4,96,1536]{2,1,0:T(8,128)(2,1)S(1)} %pad_maximum_fusion.refs_0_), channel_id=1, source_target_pairs={{0,4},{4,0},{8,12},{12,8},{16,20},{20,16},{24,28},{28,24},{1,5},{5... | collective-permute-start | bytes 3538952 | tf_op jit(solution)/shard_map/ppermute | solution.py:470
  111.5 26.4 %collective-permute-start.20 = (bf16[4,96,1536]{2,1,0:T(8,128)(2,1)}, bf16[4,96,1536]{2,1,0:T(8,128)(2,1)}, u32[]{:S(2)}, u32[]{:S(2)}) collective-permute-start(bf16[4,96,1536]{2,1,0:T(8,128)(2,1)} %collective-permute-done.12.refs_2_), channel_id=1, source_target_pairs={{0,4},{4,0},{8,12},{12,8},{16,20},{20,16},{24,28},{28,24},{1,5},{5... | collective-permute-start | bytes 3538952 | tf_op jit(solution)/shard_map/ppermute | solution.py:470
  111.9 26.1 %collective-permute-start.21 = (bf16[4,96,1536]{2,1,0:T(8,128)(2,1)}, bf16[4,96,1536]{2,1,0:T(8,128)(2,1)}, u32[]{:S(2)}, u32[]{:S(2)}) collective-permute-start(bf16[4,96,1536]{2,1,0:T(8,128)(2,1)} %collective-permute-done.13.refs_4_), channel_id=1, source_target_pairs={{0,4},{4,0},{8,12},{12,8},{16,20},{20,16},{24,28},{28,24},{1,5},{5... | collective-permute-start | bytes 3538952 | tf_op jit(solution)/shard_map/ppermute | solution.py:470
  112.1 25.9 %collective-permute-start.22 = (bf16[4,96,1536]{2,1,0:T(8,128)(2,1)}, bf16[4,96,1536]{2,1,0:T(8,128)(2,1)}, u32[]{:S(2)}, u32[]{:S(2)}) collective-permute-start(bf16[4,96,1536]{2,1,0:T(8,128)(2,1)} %collective-permute-done.14.refs_6_), channel_id=1, source_target_pairs={{0,4},{4,0},{8,12},{12,8},{16,20},{20,16},{24,28},{28,24},{1,5},{5... | collective-permute-start | bytes 3538952 | tf_op jit(solution)/shard_map/ppermute | solution.py:470
  136.8 24.7 %copy-start.19 = (f32[8,768]{1,0:T(8,128)}, f32[8,768]{1,0:T(8,128)S(1)}, u32[]{:S(2)}) copy-start(f32[8,768]{1,0:T(8,128)S(1)} %bitcast_add_fusion) | copy-start | bytes 73732
  136.8 30.4 %collective-permute-start.24 = (bf16[4,96,1536]{2,1,0:T(8,128)(2,1)}, bf16[4,96,1536]{2,1,0:T(8,128)(2,1)S(1)}, u32[]{:S(2)}, u32[]{:S(2)}) collective-permute-start(bf16[4,96,1536]{2,1,0:T(8,128)(2,1)} %get-tuple-element.148), channel_id=1, source_target_pairs={{0,4},{4,0},{8,12},{12,8},{16,20},{20,16},{24,28},{28,24},{1,5},{5... | collective-permute-start | bytes 3538952 | tf_op jit(solution)/shard_map/ppermute | solution.py:470
  138.0 29.2 %copy-start.10 = (bf16[4,96,1536]{2,1,0:T(8,128)(2,1)S(1)}, bf16[4,96,1536]{2,1,0:T(8,128)(2,1)}, u32[]{:S(2)}) copy-start(bf16[4,96,1536]{2,1,0:T(8,128)(2,1)} %get-tuple-element.147) | copy-start | bytes 3538948
  161.5 41.2 %collective-permute-start.23 = (bf16[2,512,768]{2,1,0:T(8,128)(2,1)}, bf16[2,512,768]{2,1,0:T(8,128)(2,1)S(1)}, u32[]{:S(2)}, u32[]{:S(2)}) collective-permute-start(bf16[2,512,768]{2,1,0:T(8,128)(2,1)} %get-tuple-element.146), channel_id=1, source_target_pairs={{0,1},{1,0},{2,3},{3,2},{4,5},{5,4},{6,7},{7,6},{8,9},{9,8},{10,11... | collective-permute-start | bytes 4718600 | tf_op jit(solution)/shard_map/ppermute | solution.py:470
  167.6 26.9 %collective-permute-start.25 = (bf16[96,1536]{1,0:T(8,128)(2,1)S(1)}, bf16[96,1536]{1,0:T(8,128)(2,1)S(1)}, u32[]{:S(2)}, u32[]{:S(2)}) collective-permute-start(bf16[96,1536]{1,0:T(8,128)(2,1)S(1)} %get-tuple-element.212), channel_id=1, source_target_pairs={{0,8},{4,12},{8,0},{12,4},{16,24},{20,28},{24,16},{28,20},{1,9},{5... | collective-permute-start | bytes 884744 | tf_op jit(solution)/shard_map/ppermute | solution.py:470
  168.5 26.1 %collective-permute-start.26 = (bf16[96,1536]{1,0:T(8,128)(2,1)S(1)}, bf16[96,1536]{1,0:T(8,128)(2,1)S(1)}, u32[]{:S(2)}, u32[]{:S(2)}) collective-permute-start(bf16[96,1536]{1,0:T(8,128)(2,1)S(1)} %get-tuple-element.211), channel_id=1, source_target_pairs={{0,16},{4,20},{8,24},{12,28},{16,0},{20,4},{24,8},{28,12},{1,17},{... | collective-permute-start | bytes 884744 | tf_op jit(solution)/shard_map/ppermute | solution.py:470
  169.2 25.4 %collective-permute-start.27 = (bf16[96,1536]{1,0:T(8,128)(2,1)S(1)}, bf16[96,1536]{1,0:T(8,128)(2,1)S(1)}, u32[]{:S(2)}, u32[]{:S(2)}) collective-permute-start(bf16[96,1536]{1,0:T(8,128)(2,1)S(1)} %get-tuple-element.210), channel_id=1, source_target_pairs={{0,24},{4,28},{8,16},{12,20},{16,8},{20,12},{24,0},{28,4},{1,25},{... | collective-permute-start | bytes 884744 | tf_op jit(solution)/shard_map/ppermute | solution.py:470
  194.5 43.0 %collective-permute-start.28 = (bf16[2,512,768]{2,1,0:T(8,128)(2,1)}, bf16[2,512,768]{2,1,0:T(8,128)(2,1)}, u32[]{:S(2)}, u32[]{:S(2)}) collective-permute-start(bf16[2,512,768]{2,1,0:T(8,128)(2,1)} %get-tuple-element.159), channel_id=1, source_target_pairs={{0,1},{1,0},{2,3},{3,2},{4,5},{5,4},{6,7},{7,6},{8,9},{9,8},{10,11... | collective-permute-start | bytes 4718600 | tf_op jit(solution)/shard_map/ppermute | solution.py:470
  194.5 31.6 %copy-start.14 = (bf16[96,1536]{1,0:T(8,128)(2,1)}, bf16[96,1536]{1,0:T(8,128)(2,1)S(1)}, u32[]{:S(2)}) copy-start(bf16[96,1536]{1,0:T(8,128)(2,1)S(1)} %collective-permute-done.25) | copy-start | bytes 884740
  194.6 31.6 %copy-start.15 = (bf16[96,1536]{1,0:T(8,128)(2,1)}, bf16[96,1536]{1,0:T(8,128)(2,1)S(1)}, u32[]{:S(2)}) copy-start(bf16[96,1536]{1,0:T(8,128)(2,1)S(1)} %collective-permute-done.26) | copy-start | bytes 884740
  194.6 31.6 %copy-start.16 = (bf16[96,1536]{1,0:T(8,128)(2,1)}, bf16[96,1536]{1,0:T(8,128)(2,1)S(1)}, u32[]{:S(2)}) copy-start(bf16[96,1536]{1,0:T(8,128)(2,1)S(1)} %collective-permute-done.27) | copy-start | bytes 884740
  202.7 23.5 %copy-start.3 = (bf16[2,512,768]{2,1,0:T(8,128)(2,1)}, bf16[2,512,768]{2,1,0:T(8,128)(2,1)S(1)}, u32[]{:S(2)}) copy-start(bf16[2,512,768]{2,1,0:T(8,128)(2,1)S(1)} %collective-permute-done.23) | copy-start | bytes 4718596
  202.7 23.5 %copy-start.20 = (f32[8,768]{1,0:T(8,128)S(1)}, f32[8,768]{1,0:T(8,128)}, u32[]{:S(2)}) copy-start(f32[8,768]{1,0:T(8,128)} %get-tuple-element.172) | copy-start | bytes 73732
  202.7 23.5 %copy-start.21 = (f32[8,768]{1,0:T(8,128)S(1)}, f32[8,768]{1,0:T(8,128)}, u32[]{:S(2)}) copy-start(f32[8,768]{1,0:T(8,128)} %get-tuple-element.173) | copy-start | bytes 73732
  202.7 24.3 %slice-start.2 = ((f32[8,768]{1,0:T(8,128)}), f32[2,768]{1,0:T(2,128)S(1)}, s32[]{:S(2)}) async-start(f32[8,768]{1,0:T(8,128)} %copy-done.19), calls=%async_computation.2 | async-start | bytes 12288 | tf_op jit(solution)/shard_map/slice | solution.py:609
  227.4 13.2 %collective-permute-start.32 = (f32[12,768]{1,0:T(8,128)S(1)}, f32[12,768]{1,0:T(8,128)S(1)}, u32[]{:S(2)}, u32[]{:S(2)}) collective-permute-start(f32[12,768]{1,0:T(8,128)S(1)} %concatenate.61), channel_id=1, source_target_pairs={{0,4},{4,0},{8,12},{12,8},{16,20},{20,16},{24,28},{28,24},{1,5},{5... | collective-permute-start | bytes 110600 | tf_op jit(solution)/shard_map/ppermute | solution.py:470
  227.5 13.2 %collective-permute-start.30 = (bf16[4,96,3072]{2,1,0:T(8,128)(2,1)}, bf16[4,96,3072]{2,1,0:T(8,128)(2,1)S(1)}, u32[]{:S(2)}, u32[]{:S(2)}) collective-permute-start(bf16[4,96,3072]{2,1,0:T(8,128)(2,1)} %get-tuple-element.162), channel_id=1, source_target_pairs={{0,4},{4,0},{8,12},{12,8},{16,20},{20,16},{24,28},{28,24},{1,5},{5... | collective-permute-start | bytes 7077896 | tf_op jit(solution)/shard_map/ppermute | solution.py:470
  228.0 42.2 %collective-permute-start.29 = (bf16[2,512,768]{2,1,0:T(8,128)(2,1)}, bf16[2,512,768]{2,1,0:T(8,128)(2,1)}, u32[]{:S(2)}, u32[]{:S(2)}) collective-permute-start(bf16[2,512,768]{2,1,0:T(8,128)(2,1)} %get-tuple-element.160), channel_id=1, source_target_pairs={{0,1},{1,0},{2,3},{3,2},{4,5},{5,4},{6,7},{7,6},{8,9},{9,8},{10,11... | collective-permute-start | bytes 4718600 | tf_op jit(solution)/shard_map/ppermute | solution.py:470
  233.9 2.6 copy-start.6
  236.5 3.0 %copy-start.8 = (bf16[2,512,768]{2,1,0:T(8,128)(2,1)S(1)}, bf16[2,512,768]{2,1,0:T(8,128)(2,1)}, u32[]{:S(2)}) copy-start(bf16[2,512,768]{2,1,0:T(8,128)(2,1)} %get-tuple-element.160) | copy-start | bytes 4718596
  244.4 31.9 %collective-permute-start.33 = (bf16[104,3072]{1,0:T(8,128)(2,1)}, bf16[104,3072]{1,0:T(8,128)(2,1)S(1)}, u32[]{:S(2)}, u32[]{:S(2)}) collective-permute-start(bf16[104,3072]{1,0:T(8,128)(2,1)} %get-tuple-element.228), channel_id=1, source_target_pairs={{0,8},{4,12},{8,0},{12,4},{16,24},{20,28},{24,16},{28,20},{1,9},{5... | collective-permute-start | bytes 1916936 | tf_op jit(solution)/shard_map/ppermute | solution.py:470
  245.2 31.1 %collective-permute-start.34 = (bf16[104,3072]{1,0:T(8,128)(2,1)S(1)}, bf16[104,3072]{1,0:T(8,128)(2,1)S(1)}, u32[]{:S(2)}, u32[]{:S(2)}) collective-permute-start(bf16[104,3072]{1,0:T(8,128)(2,1)S(1)} %get-tuple-element.229), channel_id=1, source_target_pairs={{0,16},{4,20},{8,24},{12,28},{16,0},{20,4},{24,8},{28,12},{1,17},{... | collective-permute-start | bytes 1916936 | tf_op jit(solution)/shard_map/ppermute | solution.py:470
  245.9 30.4 %collective-permute-start.35 = (bf16[104,3072]{1,0:T(8,128)(2,1)S(1)}, bf16[104,3072]{1,0:T(8,128)(2,1)}, u32[]{:S(2)}, u32[]{:S(2)}) collective-permute-start(bf16[104,3072]{1,0:T(8,128)(2,1)S(1)} %get-tuple-element.230), channel_id=1, source_target_pairs={{0,24},{4,28},{8,16},{12,20},{16,8},{20,12},{24,0},{28,4},{1,25},{... | collective-permute-start | bytes 1916936 | tf_op jit(solution)/shard_map/ppermute | solution.py:470
  247.9 5.5 %slice-start = ((s8[4718592]{0:T(1024)(128)(4,1)}), s8[4194304]{0:T(1024)(128)(4,1)S(1)}, s32[]{:S(2)}) async-start(s8[4718592]{0:T(1024)(128)(4,1)} %bitcast.100), calls=%async_computation | async-start | bytes 8388608
  247.9 5.5 %slice-start.1 = ((s8[4718592]{0:T(1024)(128)(4,1)}), s8[524288]{0:T(1024)(128)(4,1)S(1)}, s32[]{:S(2)}) async-start(s8[4718592]{0:T(1024)(128)(4,1)} %bitcast.100), calls=%async_computation.1 | async-start | bytes 1048576
  248.0 5.5 %copy-start.2 = (bf16[2,512,768]{2,1,0:T(8,128)(2,1)S(1)}, bf16[2,512,768]{2,1,0:T(8,128)(2,1)}, u32[]{:S(2)}) copy-start(bf16[2,512,768]{2,1,0:T(8,128)(2,1)} %get-tuple-element.146) | copy-start | bytes 4718596
  248.0 26.7 %collective-permute-start.31 = (bf16[96,768]{1,0:T(8,128)(2,1)S(1)}, bf16[96,768]{1,0:T(8,128)(2,1)S(1)}, u32[]{:S(2)}, u32[]{:S(2)}) collective-permute-start(bf16[96,768]{1,0:T(8,128)(2,1)S(1)} %broadcast_select_fusion), channel_id=1, source_target_pairs={{0,1},{1,0},{2,3},{3,2},{4,5},{5,4},{6,7},{7,6},{8,9},{9,8},{10,11... | collective-permute-start | bytes 442376 | tf_op jit(solution)/shard_map/ppermute | solution.py:470
  278.1 3.8 %collective-permute-start.36 = (f32[12,96]{1,0:T(8,128)S(1)}, f32[12,96]{1,0:T(8,128)S(1)}, u32[]{:S(2)}, u32[]{:S(2)}) collective-permute-start(f32[12,96]{1,0:T(8,128)S(1)} %pad_maximum_fusion.5), channel_id=1, source_target_pairs={{0,1},{1,0},{2,3},{3,2},{4,5},{5,4},{6,7},{7,6},{8,9},{9,8},{10,11... | collective-permute-start | bytes 13832 | tf_op jit(solution)/shard_map/ppermute | solution.py:470
  280.1 7.8 %collective-permute-start.37 = (bf16[96,1536]{1,0:T(8,128)(2,1)S(1)}, bf16[96,1536]{1,0:T(8,128)(2,1)S(1)}, u32[]{:S(2)}, u32[]{:S(2)}) collective-permute-start(bf16[96,1536]{1,0:T(8,128)(2,1)S(1)} %pad_maximum_fusion.4), channel_id=1, source_target_pairs={{0,1},{1,0},{2,3},{3,2},{4,5},{5,4},{6,7},{7,6},{8,9},{9,8},{10,11... | collective-permute-start | bytes 884744 | tf_op jit(solution)/shard_map/ppermute | solution.py:470
  282.5 6.9 %copy-start.25 = (f32[96]{0:T(128)}, f32[96]{0:T(128)S(1)}, u32[]{:S(2)}) copy-start(f32[96]{0:T(128)S(1)} %get-tuple-element.263) | copy-start | bytes 1156
  (5 other events, 10.7 us)
where the time goes:
time: 293 us; the launch traced here: 290 us
  Pallas kernels  144 us (49%)
  waiting for transfers between devices  50 us (17%)
  starting transfers between devices  43.8 us (15%)
  local copies, waits for them, and re-layouts  26 us (9%)
  other arithmetic  23.9 us (8%)
    pallas_call x3, Pallas kernels, feed(): pl.pallas_call(functools.partial(feed_kernel, pieces=pieces, earlier=1 if...  70.2 us
    pallas_call x2, Pallas kernels, attention(): pl.pallas_call(functools.partial(attention_kernel, pieces=pieces, earlier...  66.7 us
    ppermute x38, waiting for transfers between devices, trade(): return lax.ppermute(array, axis, [(i, i ^ mask) for i in range(size)])  50 us
    ppermute x38, starting transfers between devices, trade(): return lax.ppermute(array, axis, [(i, i ^ mask) for i in range(size)])  43.8 us
    dynamic_update_slice x6, other arithmetic, body(): lax.dynamic_update_slice(input_grad, item[1].astype(F32) + given.astype(F...  10.2 us
    dynamic_update_slice x6, local copies, waits for them, and re-layouts, body(): layer_output = lax.dynamic_update_slice(layer_output, item[0], (at, 0))  7.84 us
    pallas_call x1, Pallas kernels, prepare(): pl.pallas_call(functools.partial(prepare_kernel, part=part), grid_spec=pl...  7.43 us
  transfers between devices with their start and end apart: 38, of which 13 were waited for; matrix products, arithmetic and copies ran while one was open for 14% of the time, Pallas kernels for 50%

commit v1 on v0

--- a/solution.py
+++ b/solution.py
@@ -595,6 +595,9 @@
             if fast:
                 heads_items = exchange_across(heads_part)
                 wait = wait, heads_items
+            blank = jnp.zeros(block_input.shape, BF16), jnp.zeros(block_input.shape, F32)
+            blank = tie(blank, done[1])
+            wait = wait, blank
     if fast:
         heads_cols = add_up(tie(heads_items, done[1])).astype(BF16)
     else:
@@ -654,8 +657,7 @@
     left, right = heads_cols[:, :half], heads_cols[:, half:]
     heads_sum = settle(jnp.where(odd == 0, left, right), jnp.where(odd == 0, right, left))
 
-    layer_output = tie(jnp.zeros(block_input.shape, BF16), done[1])
-    input_grad = tie(jnp.zeros(block_input.shape, F32), ready)
+    layer_output, input_grad = tie(blank[0], done[1]), tie(blank[1], ready)
     for i, both in enumerate(others):
         for item, base in zip(both, (odd, 1 - odd)):
             at = (base * count + i) * SEQ

time: 293 us -> 293 us (level)
  no operation moved by 1% of the time
where the time goes in v1:
time: 293 us; the launch traced here: 290 us
  Pallas kernels  144 us (49%)
  waiting for transfers between devices  50 us (17%)
  starting transfers between devices  43.8 us (15%)
  local copies, waits for them, and re-layouts  26 us (9%)
  other arithmetic  23.9 us (8%)
    pallas_call x3, Pallas kernels, feed(): pl.pallas_call(functools.partial(feed_kernel, pieces=pieces, earlier=1 if...  70.2 us
    pallas_call x2, Pallas kernels, attention(): pl.pallas_call(functools.partial(attention_kernel, pieces=pieces, earlier...  66.7 us
    ppermute x38, waiting for transfers between devices, trade(): return lax.ppermute(array, axis, [(i, i ^ mask) for i in range(size)])  50 us
    ppermute x38, starting transfers between devices, trade(): return lax.ppermute(array, axis, [(i, i ^ mask) for i in range(size)])  43.8 us
    dynamic_update_slice x6, other arithmetic, body(): lax.dynamic_update_slice(input_grad, item[1].astype(F32) + given.astype(F...  10.2 us
    dynamic_update_slice x6, local copies, waits for them, and re-layouts, body(): layer_output = lax.dynamic_update_slice(layer_output, item[0], (at, 0))  7.84 us
    pallas_call x1, Pallas kernels, prepare(): pl.pallas_call(functools.partial(prepare_kernel, part=part), grid_spec=pl...  7.43 us
  transfers between devices with their start and end apart: 38, of which 13 were waited for; matrix products, arithmetic and copies ran while one was open for 14% of the time, Pallas kernels for 50%

profile of v1, /device:TPU:0, one launch (start us, length us, event | category | flops | bytes accessed | tf_op | source)
XLA Modules:
  0.0 289.6 jit_solution(4742644584812386259)
XLA Ops:
  0.7 0.9 copy.44
  2.3 0.8 stack.86
  3.2 1.0 fusion.22
  4.2 3.0 %collective-permute-start.3 = (bf16[1,96,896]{2,1,0:T(8,128)(2,1)S(1)}, bf16[1,96,896]{2,1,0:T(8,128)(2,1)S(1)}, u32[]{:S(2)}, u32[]{:S(2)}) collective-permute-start(bf16[1,96,896]{2,1,0:T(8,128)(2,1)S(1)} %fusion.22), channel_id=1, source_target_pairs={{0,8},{4,12},{8,0},{12,4},{16,24},{20,28},{24,16},{28,20},{1,9},{5... | collective-permute-start | bytes 516104 | tf_op jit(solution)/shard_map/ppermute | solution.py:470
  7.2 1.5 collective-permute-start.4
  8.7 1.0 fusion.14
  9.7 2.1 collective-permute-start
  11.8 2.6 collective-permute-start.1
  14.4 2.1 collective-permute-start.2
  16.7 0.7 collective-permute-done
  17.4 9.5 %collective-permute-done.1 = bf16[96,896]{1,0:T(8,128)(2,1)S(1)} collective-permute-done((bf16[96,896]{1,0:T(8,128)(2,1)S(1)}, bf16[96,896]{1,0:T(8,128)(2,1)S(1)}, u32[]{:S(2)}, u32[]{:S(2)}) %collective-permute-start.1) | collective-permute-done | bytes 172064 | tf_op jit(solution)/shard_map/ppermute | solution.py:470
  27.0 2.5 collective-permute-start.11
  29.6 2.5 collective-permute-start.6
  32.0 1.1 collective-permute-start.7
  35.0 7.5 %collective-permute-done.6 = bf16[96,1536]{1,0:T(8,128)(2,1)S(1)} collective-permute-done((bf16[96,1536]{1,0:T(8,128)(2,1)S(1)}, bf16[96,1536]{1,0:T(8,128)(2,1)S(1)}, u32[]{:S(2)}, u32[]{:S(2)}) %collective-permute-start.6) | collective-permute-done | bytes 294944 | tf_op jit(solution)/shard_map/ppermute | solution.py:470
  42.6 1.6 collective-permute-start.8
  44.2 0.8 constant_dynamic-update-slice_fusion.4.refs_6_
  45.0 3.4 %collective-permute-done.10 = bf16[3,96,896]{2,1,0:T(8,128)(2,1)S(1)} collective-permute-done((bf16[3,96,896]{2,1,0:T(8,128)(2,1)S(1)}, bf16[3,96,896]{2,1,0:T(8,128)(2,1)S(1)}, u32[]{:S(2)}, u32[]{:S(2)}) %collective-permute-start.10) | collective-permute-done | bytes 516128 | tf_op jit(solution)/shard_map/ppermute | solution.py:470
  48.6 5.0 %collective-permute-done.7 = bf16[96,1536]{1,0:T(8,128)(2,1)S(1)} collective-permute-done((bf16[96,1536]{1,0:T(8,128)(2,1)S(1)}, bf16[96,1536]{1,0:T(8,128)(2,1)S(1)}, u32[]{:S(2)}, u32[]{:S(2)}) %collective-permute-start.7) | collective-permute-done | bytes 294944 | tf_op jit(solution)/shard_map/ppermute | solution.py:470
  57.1 1.5 collective-permute-start.14
  59.1 7.4 %prepare.1 = (bf16[2304,768]{1,0:T(8,128)(2,1)}, bf16[768,768]{1,0:T(8,128)(2,1)}, f32[4,8,768]{2,1,0:T(8,128)}, f32[4,8,576]{2,1,0:T(8,128)}) custom-call(s32[5]{0:T(128)} %copy-done.22, bf16[4,96,896]{2,1,0:T(8,128)(2,1)} %copy-done, bf16[4,96,896]{2,1,0:T(8,128)(2,1)} %collective-permute-done.15.refs_1_, bf16[4,96,896]{2,1,0:T(8,128)(2,1)} %copy-done.12, ...), custom_call_target="tpu_custom_call" | custom-call | tf_op jit(solution)/shard_map/prepare/pallas_call | solution.py:440
  66.5 43.1 %attention.2 = (bf16[1024,768]{1,0:T(8,128)(2,1)}, bf16[1024,768]{1,0:T(8,128)(2,1)}, f32[2,8,768]{2,1,0:T(8,128)}, f32[2,8,1152]{2,1,0:T(8,128)}, bf16[4,96,153...) custom-call(s32[5]{0:T(128)} %copy-done.27, bf16[3072,768]{1,0:T(8,128)(2,1)} %x_ref.9, bf16[3072,768]{1,0:T(8,128)(2,1)} %g_ref.9, ...), custom_call_target="tpu_custom_call" | custom-call | flops 32000000000 | bytes 24000000 | tf_op jit(solution)/shard_map/attention/pallas_call | solution.py:349
  109.6 0.9 reduce_sum.32
  110.5 0.8 reduce_sum.23
  112.4 23.6 %attention.3 = (bf16[512,768]{1,0:T(8,128)(2,1)}, bf16[512,768]{1,0:T(8,128)(2,1)}, f32[1,8,768]{2,1,0:T(8,128)}, f32[1,8,1152]{2,1,0:T(8,128)}, bf16[4,96,1536]...) custom-call(s32[5]{0:T(128)} %copy-done.26, bf16[3072,768]{1,0:T(8,128)(2,1)} %x_ref.9, bf16[3072,768]{1,0:T(8,128)(2,1)} %g_ref.9, ...), custom_call_target="tpu_custom_call" | custom-call | flops 16000000000 | bytes 12000000 | tf_op jit(solution)/shard_map/attention/pallas_call | solution.py:349
  136.1 0.7 bitcast_add_fusion
  137.0 0.8 fusion.15
  138.0 23.5 %feed.3 = (f32[8,768]{1,0:T(8,128)}, bf16[2,512,768]{2,1,0:T(8,128)(2,1)}, bf16[4,96,3072]{2,1,0:T(8,128)(2,1)}, bf16[4,96,3072]{2,1,0:T(8,128)(2,1)}) custom-call(s32[5]{0:T(128)} %copy-done.27, bf16[3072,768]{1,0:T(8,128)(2,1)} %x_ref.9, bf16[3072,768]{1,0:T(8,128)(2,1)} %g_ref.9, f32[4,8,768]{2,1,0:T(8,128)} %get-tuple-element.136.vec_ref.bias_ref, ...), custom_call_target="tpu_custom_call" | custom-call | flops 16000000000 | bytes 9000000 | tf_op jit(solution)/shard_map/feed/pallas_call | solution.py:394
  161.5 5.7 %collective-permute-start.24 = (bf16[2,512,768]{2,1,0:T(8,128)(2,1)}, bf16[2,512,768]{2,1,0:T(8,128)(2,1)S(1)}, u32[]{:S(2)}, u32[]{:S(2)}) collective-permute-start(bf16[2,512,768]{2,1,0:T(8,128)(2,1)} %get-tuple-element.155), channel_id=1, source_target_pairs={{0,1},{1,0},{2,3},{3,2},{4,5},{5,4},{6,7},{7,6},{8,9},{9,8},{10,11... | collective-permute-start | bytes 4718600 | tf_op jit(solution)/shard_map/ppermute | solution.py:470
  167.6 0.8 collective-permute-start.25
  169.2 2.0 collective-permute-start.27
  171.2 23.3 %feed.4 = (f32[8,768]{1,0:T(8,128)}, bf16[2,512,768]{2,1,0:T(8,128)(2,1)}, bf16[4,96,3072]{2,1,0:T(8,128)(2,1)}, bf16[4,96,3072]{2,1,0:T(8,128)(2,1)}) custom-call(s32[5]{0:T(128)} %copy-done.24, bf16[3072,768]{1,0:T(8,128)(2,1)} %x_ref.9, bf16[3072,768]{1,0:T(8,128)(2,1)} %g_ref.9, ...), custom_call_target="tpu_custom_call", output_to_operand_aliasing={{2}: (15, {}), {3}: (16, {})} | custom-call | flops 16000000000 | bytes 9000000 | tf_op jit(solution)/shard_map/feed/pallas_call | solution.py:394
  194.6 8.1 %collective-permute-done.24 = bf16[2,512,768]{2,1,0:T(8,128)(2,1)S(1)} collective-permute-done((bf16[2,512,768]{2,1,0:T(8,128)(2,1)}, bf16[2,512,768]{2,1,0:T(8,128)(2,1)S(1)}, u32[]{:S(2)}, u32[]{:S(2)}) %collective-permute-start.24) | collective-permute-done | bytes 1572896 | tf_op jit(solution)/shard_map/ppermute | solution.py:470
  202.7 23.4 %feed.5 = (f32[8,768]{1,0:T(8,128)}, bf16[2,512,768]{2,1,0:T(8,128)(2,1)}, bf16[4,96,3072]{2,1,0:T(8,128)(2,1)}, bf16[4,96,3072]{2,1,0:T(8,128)(2,1)}) custom-call(s32[5]{0:T(128)} %copy-done.26, bf16[3072,768]{1,0:T(8,128)(2,1)} %x_ref.9, bf16[3072,768]{1,0:T(8,128)(2,1)} %g_ref.9, ...), custom_call_target="tpu_custom_call", output_to_operand_aliasing={{2}: (15, {}), {3}: (16, {})} | custom-call | flops 16000000000 | bytes 9000000 | tf_op jit(solution)/shard_map/feed/pallas_call | solution.py:394
  226.2 0.7 add_add_fusion
  228.0 2.0 collective-permute-start.29
  230.0 1.3 add_convert_fusion.2
  231.4 2.5 broadcast_in_dim.12
  233.9 0.9 bitcast_dynamic-update-slice_fusion.3
  234.8 0.8 copy-done.4
  235.6 0.9 fusion.8
  236.5 0.9 bitcast_dynamic-update-slice_fusion.2
  237.4 2.1 fusion.7
  239.5 0.9 bitcast_dynamic-update-slice_fusion.1
  240.7 2.6 add_convert_fusion
  243.4 1.0 fusion.10
  244.4 0.8 collective-permute-start.33
  245.9 2.0 collective-permute-start.35
  248.0 1.1 collective-permute-start.31
  249.1 4.3 %broadcast_in_dim.13 = f32[3072,768]{1,0:T(8,128)} broadcast(f32[]{:T(128)} %constant.143.clone.1), dimensions={} | broadcast | bytes 9437188 | tf_op jit(solution)/shard_map/broadcast_in_dim | solution.py:598
  253.4 1.3 fusion.5
  255.4 1.3 fusion.4
  257.4 1.3 fusion.3
  258.7 2.6 fusion.2
  261.3 1.3 fusion.1
  262.5 7.6 %collective-permute-done.29 = bf16[2,512,768]{2,1,0:T(8,128)(2,1)} collective-permute-done((bf16[2,512,768]{2,1,0:T(8,128)(2,1)}, bf16[2,512,768]{2,1,0:T(8,128)(2,1)}, u32[]{:S(2)}, u32[]{:S(2)}) %collective-permute-start.29) | collective-permute-done | bytes 1572896 | tf_op jit(solution)/shard_map/ppermute | solution.py:470
  270.2 2.4 fusion
  272.6 2.1 bitcast_dynamic-update-slice_fusion
  275.5 0.7 copy.46
  276.3 1.5 fusion.16
  278.1 2.0 collective-permute-start.36
  280.2 1.6 collective-permute-done.36
  283.0 4.9 %collective-permute-done.37 = bf16[96,1536]{1,0:T(8,128)(2,1)S(1)} collective-permute-done((bf16[96,1536]{1,0:T(8,128)(2,1)S(1)}, bf16[96,1536]{1,0:T(8,128)(2,1)S(1)}, u32[]{:S(2)}, u32[]{:S(2)}) %collective-permute-start.37) | collective-permute-done | bytes 294944 | tf_op jit(solution)/shard_map/ppermute | solution.py:470
  288.0 0.9 slice_bitcast_fusion.8
  (159 shorter events, 16.1 us)
Async XLA Ops:
  0.6 28.9 %copy-start.17 = (bf16[768,96]{0,1:T(8,128)(2,1)S(1)}, bf16[768,96]{0,1:T(8,128)(2,1)}, u32[]{:S(2)}) copy-start(bf16[768,96]{0,1:T(8,128)(2,1)} %param.34) | copy-start | bytes 442372
  0.7 28.9 %copy-start.18 = (bf16[96,768]{1,0:T(8,128)(2,1)S(1)}, bf16[96,768]{1,0:T(8,128)(2,1)}, u32[]{:S(2)}) copy-start(bf16[96,768]{1,0:T(8,128)(2,1)} %param.32) | copy-start | bytes 442372
  4.2 10.2 %collective-permute-start.3 = (bf16[1,96,896]{2,1,0:T(8,128)(2,1)S(1)}, bf16[1,96,896]{2,1,0:T(8,128)(2,1)S(1)}, u32[]{:S(2)}, u32[]{:S(2)}) collective-permute-start(bf16[1,96,896]{2,1,0:T(8,128)(2,1)S(1)} %fusion.22), channel_id=1, source_target_pairs={{0,8},{4,12},{8,0},{12,4},{16,24},{20,28},{24,16},{28,20},{1,9},{5... | collective-permute-start | bytes 516104 | tf_op jit(solution)/shard_map/ppermute | solution.py:470
  7.2 9.5 %collective-permute-start.4 = (bf16[1,96,896]{2,1,0:T(8,128)(2,1)S(1)}, bf16[1,96,896]{2,1,0:T(8,128)(2,1)S(1)}, u32[]{:S(2)}, u32[]{:S(2)}) collective-permute-start(bf16[1,96,896]{2,1,0:T(8,128)(2,1)S(1)} %fusion.22), channel_id=1, source_target_pairs={{0,16},{4,20},{8,24},{12,28},{16,0},{20,4},{24,8},{28,12},{1,17},{... | collective-permute-start | bytes 516104 | tf_op jit(solution)/shard_map/ppermute | solution.py:470
  8.7 8.0 %collective-permute-start.5 = (bf16[1,96,896]{2,1,0:T(8,128)(2,1)S(1)}, bf16[1,96,896]{2,1,0:T(8,128)(2,1)S(1)}, u32[]{:S(2)}, u32[]{:S(2)}) collective-permute-start(bf16[1,96,896]{2,1,0:T(8,128)(2,1)S(1)} %fusion.22), channel_id=1, source_target_pairs={{0,24},{4,28},{8,16},{12,20},{16,8},{20,12},{24,0},{28,4},{1,25},{... | collective-permute-start | bytes 516104 | tf_op jit(solution)/shard_map/ppermute | solution.py:470
  9.7 7.7 %collective-permute-start = (bf16[96,896]{1,0:T(8,128)(2,1)S(1)}, bf16[96,896]{1,0:T(8,128)(2,1)S(1)}, u32[]{:S(2)}, u32[]{:S(2)}) collective-permute-start(bf16[96,896]{1,0:T(8,128)(2,1)S(1)} %fusion.14), channel_id=1, source_target_pairs={{0,1},{1,0},{2,3},{3,2},{4,5},{5,4},{6,7},{7,6},{8,9},{9,8},{10,11... | collective-permute-start | bytes 516104 | tf_op jit(solution)/shard_map/ppermute | solution.py:470
  11.8 15.2 %collective-permute-start.1 = (bf16[96,896]{1,0:T(8,128)(2,1)S(1)}, bf16[96,896]{1,0:T(8,128)(2,1)S(1)}, u32[]{:S(2)}, u32[]{:S(2)}) collective-permute-start(bf16[96,896]{1,0:T(8,128)(2,1)S(1)} %fusion.14), channel_id=1, source_target_pairs={{0,2},{1,3},{2,0},{3,1},{4,6},{5,7},{6,4},{7,5},{8,10},{9,11},{10,... | collective-permute-start | bytes 516104 | tf_op jit(solution)/shard_map/ppermute | solution.py:470
  14.4 12.6 %collective-permute-start.2 = (bf16[96,896]{1,0:T(8,128)(2,1)S(1)}, bf16[96,896]{1,0:T(8,128)(2,1)S(1)}, u32[]{:S(2)}, u32[]{:S(2)}) collective-permute-start(bf16[96,896]{1,0:T(8,128)(2,1)S(1)} %fusion.14), channel_id=1, source_target_pairs={{0,3},{1,2},{2,1},{3,0},{4,7},{5,6},{6,5},{7,4},{8,11},{9,10},{10,... | collective-permute-start | bytes 516104 | tf_op jit(solution)/shard_map/ppermute | solution.py:470
  27.0 17.2 %collective-permute-start.11 = (bf16[3,96,896]{2,1,0:T(8,128)(2,1)S(1)}, bf16[3,96,896]{2,1,0:T(8,128)(2,1)S(1)}, u32[]{:S(2)}, u32[]{:S(2)}) collective-permute-start(bf16[3,96,896]{2,1,0:T(8,128)(2,1)S(1)} %pad_maximum_fusion.2), channel_id=1, source_target_pairs={{0,24},{4,28},{8,16},{12,20},{16,8},{20,12},{24,0},{28,4},{1,25},{... | collective-permute-start | bytes 1548296 | tf_op jit(solution)/shard_map/ppermute | solution.py:470
  29.6 13.0 %collective-permute-start.6 = (bf16[96,1536]{1,0:T(8,128)(2,1)S(1)}, bf16[96,1536]{1,0:T(8,128)(2,1)S(1)}, u32[]{:S(2)}, u32[]{:S(2)}) collective-permute-start(bf16[96,1536]{1,0:T(8,128)(2,1)S(1)} %pad_maximum_fusion.3), channel_id=1, source_target_pairs={{0,1},{1,0},{2,3},{3,2},{4,5},{5,4},{6,7},{7,6},{8,9},{9,8},{10,11... | collective-permute-start | bytes 884744 | tf_op jit(solution)/shard_map/ppermute | solution.py:470
  32.0 21.5 %collective-permute-start.7 = (bf16[96,1536]{1,0:T(8,128)(2,1)S(1)}, bf16[96,1536]{1,0:T(8,128)(2,1)S(1)}, u32[]{:S(2)}, u32[]{:S(2)}) collective-permute-start(bf16[96,1536]{1,0:T(8,128)(2,1)S(1)} %pad_maximum_fusion.3), channel_id=1, source_target_pairs={{0,2},{1,3},{2,0},{3,1},{4,6},{5,7},{6,4},{7,5},{8,10},{9,11},{10,... | collective-permute-start | bytes 884744 | tf_op jit(solution)/shard_map/ppermute | solution.py:470
  33.1 15.3 %collective-permute-start.10 = (bf16[3,96,896]{2,1,0:T(8,128)(2,1)S(1)}, bf16[3,96,896]{2,1,0:T(8,128)(2,1)S(1)}, u32[]{:S(2)}, u32[]{:S(2)}) collective-permute-start(bf16[3,96,896]{2,1,0:T(8,128)(2,1)S(1)} %pad_maximum_fusion.2), channel_id=1, source_target_pairs={{0,16},{4,20},{8,24},{12,28},{16,0},{20,4},{24,8},{28,12},{1,17},{... | collective-permute-start | bytes 1548296 | tf_op jit(solution)/shard_map/ppermute | solution.py:470
  33.6 14.9 %collective-permute-start.9 = (bf16[3,96,896]{2,1,0:T(8,128)(2,1)S(1)}, bf16[3,96,896]{2,1,0:T(8,128)(2,1)S(1)}, u32[]{:S(2)}, u32[]{:S(2)}) collective-permute-start(bf16[3,96,896]{2,1,0:T(8,128)(2,1)S(1)} %pad_maximum_fusion.2), channel_id=1, source_target_pairs={{0,8},{4,12},{8,0},{12,4},{16,24},{20,28},{24,16},{28,20},{1,9},{5... | collective-permute-start | bytes 1548296 | tf_op jit(solution)/shard_map/ppermute | solution.py:470
  35.0 19.4 %copy-start = (bf16[4,96,896]{2,1,0:T(8,128)(2,1)}, bf16[4,96,896]{2,1,0:T(8,128)(2,1)S(1)}, u32[]{:S(2)}) copy-start(bf16[4,96,896]{2,1,0:T(8,128)(2,1)S(1)} %pad_maximum_fusion.1.refs_0_) | copy-start | bytes 2064388
  42.6 11.0 %collective-permute-start.8 = (bf16[96,1536]{1,0:T(8,128)(2,1)S(1)}, bf16[96,1536]{1,0:T(8,128)(2,1)S(1)}, u32[]{:S(2)}, u32[]{:S(2)}) collective-permute-start(bf16[96,1536]{1,0:T(8,128)(2,1)S(1)} %pad_maximum_fusion.3), channel_id=1, source_target_pairs={{0,3},{1,2},{2,1},{3,0},{4,7},{5,6},{6,5},{7,4},{8,11},{9,10},{10,... | collective-permute-start | bytes 884744 | tf_op jit(solution)/shard_map/ppermute | solution.py:470
  48.5 5.3 %copy-start.13 = (bf16[4,96,896]{2,1,0:T(8,128)(2,1)}, bf16[4,96,896]{2,1,0:T(8,128)(2,1)S(1)}, u32[]{:S(2)}) copy-start(bf16[4,96,896]{2,1,0:T(8,128)(2,1)S(1)} %constant_dynamic-update-slice_fusion.2.refs_4_) | copy-start | bytes 2064388
  48.6 10.5 %copy-start.12 = (bf16[4,96,896]{2,1,0:T(8,128)(2,1)}, bf16[4,96,896]{2,1,0:T(8,128)(2,1)S(1)}, u32[]{:S(2)}) copy-start(bf16[4,96,896]{2,1,0:T(8,128)(2,1)S(1)} %constant_dynamic-update-slice_fusion.refs_2_) | copy-start | bytes 2064388
  53.7 57.6 %copy-start.11 = (bf16[4,96,1536]{2,1,0:T(8,128)(2,1)}, bf16[4,96,1536]{2,1,0:T(8,128)(2,1)S(1)}, u32[]{:S(2)}) copy-start(bf16[4,96,1536]{2,1,0:T(8,128)(2,1)S(1)} %pad_maximum_fusion.refs_0_) | copy-start | bytes 3538948
  53.8 2.6 collective-permute-start.18
  53.8 3.2 %collective-permute-start.17 = (bf16[4,96,896]{2,1,0:T(8,128)(2,1)S(1)}, bf16[4,96,896]{2,1,0:T(8,128)(2,1)}, u32[]{:S(2)}, u32[]{:S(2)}) collective-permute-start(bf16[4,96,896]{2,1,0:T(8,128)(2,1)S(1)} %constant_dynamic-update-slice_fusion.2.refs_4_), channel_id=1, source_target_pairs={{0,4},{4,0},{8,12},{12,8},{16,20},{20,16},{24,28},{28,24},{1,5},{5... | collective-permute-start | bytes 2064392 | tf_op jit(solution)/shard_map/ppermute | solution.py:470
  54.3 4.3 %collective-permute-start.16 = (bf16[4,96,896]{2,1,0:T(8,128)(2,1)S(1)}, bf16[4,96,896]{2,1,0:T(8,128)(2,1)}, u32[]{:S(2)}, u32[]{:S(2)}) collective-permute-start(bf16[4,96,896]{2,1,0:T(8,128)(2,1)S(1)} %constant_dynamic-update-slice_fusion.refs_2_), channel_id=1, source_target_pairs={{0,4},{4,0},{8,12},{12,8},{16,20},{20,16},{24,28},{28,24},{1,5},{5... | collective-permute-start | bytes 2064392 | tf_op jit(solution)/shard_map/ppermute | solution.py:470
  54.4 4.6 %collective-permute-start.15 = (bf16[4,96,896]{2,1,0:T(8,128)(2,1)S(1)}, bf16[4,96,896]{2,1,0:T(8,128)(2,1)}, u32[]{:S(2)}, u32[]{:S(2)}) collective-permute-start(bf16[4,96,896]{2,1,0:T(8,128)(2,1)S(1)} %pad_maximum_fusion.1.refs_0_), channel_id=1, source_target_pairs={{0,4},{4,0},{8,12},{12,8},{16,20},{20,16},{24,28},{28,24},{1,5},{5... | collective-permute-start | bytes 2064392 | tf_op jit(solution)/shard_map/ppermute | solution.py:470
  54.9 4.1 %copy-start.22 = (s32[5]{0:T(128)}, s32[5]{0:T(128)S(1)}, u32[]{:S(2)}) copy-start(s32[5]{0:T(128)S(1)} %stack.77.place) | copy-start | bytes 64
  55.0 11.5 %copy-start.27 = (s32[5]{0:T(128)}, s32[5]{0:T(128)S(1)}, u32[]{:S(2)}) copy-start(s32[5]{0:T(128)S(1)} %constant_dynamic-update-slice_fusion.6.place) | copy-start | bytes 64
  55.0 11.5 %copy-start.26 = (s32[5]{0:T(128)}, s32[5]{0:T(128)S(1)}, u32[]{:S(2)}) copy-start(s32[5]{0:T(128)S(1)} %constant_dynamic-update-slice_fusion.7.place) | copy-start | bytes 64
  55.1 56.3 %collective-permute-start.12 = (bf16[4,96,1536]{2,1,0:T(8,128)(2,1)S(1)}, bf16[4,96,1536]{2,1,0:T(8,128)(2,1)}, u32[]{:S(2)}, u32[]{:S(2)}) collective-permute-start(bf16[4,96,1536]{2,1,0:T(8,128)(2,1)S(1)} %pad_maximum_fusion.refs_0_), channel_id=1, source_target_pairs={{0,8},{4,12},{8,0},{12,4},{16,24},{20,28},{24,16},{28,20},{1,9},{5... | collective-permute-start | bytes 3538952 | tf_op jit(solution)/shard_map/ppermute | solution.py:470
  56.4 54.9 %collective-permute-start.13 = (bf16[4,96,1536]{2,1,0:T(8,128)(2,1)S(1)}, bf16[4,96,1536]{2,1,0:T(8,128)(2,1)}, u32[]{:S(2)}, u32[]{:S(2)}) collective-permute-start(bf16[4,96,1536]{2,1,0:T(8,128)(2,1)S(1)} %pad_maximum_fusion.refs_0_), channel_id=1, source_target_pairs={{0,16},{4,20},{8,24},{12,28},{16,0},{20,4},{24,8},{28,12},{1,17},{... | collective-permute-start | bytes 3538952 | tf_op jit(solution)/shard_map/ppermute | solution.py:470
  57.1 54.3 %collective-permute-start.14 = (bf16[4,96,1536]{2,1,0:T(8,128)(2,1)S(1)}, bf16[4,96,1536]{2,1,0:T(8,128)(2,1)}, u32[]{:S(2)}, u32[]{:S(2)}) collective-permute-start(bf16[4,96,1536]{2,1,0:T(8,128)(2,1)S(1)} %pad_maximum_fusion.refs_0_), channel_id=1, source_target_pairs={{0,24},{4,28},{8,16},{12,20},{16,8},{20,12},{24,0},{28,4},{1,25},{... | collective-permute-start | bytes 3538952 | tf_op jit(solution)/shard_map/ppermute | solution.py:470
  66.5 43.1 %copy-start.23 = (s32[5]{0:T(128)S(1)}, s32[5]{0:T(128)}, u32[]{:S(2)}) copy-start(s32[5]{0:T(128)} %copy-done.22) | copy-start | bytes 64
  109.6 26.5 %copy-start.24 = (s32[5]{0:T(128)}, s32[5]{0:T(128)S(1)}, u32[]{:S(2)}) copy-start(s32[5]{0:T(128)S(1)} %constant_dynamic-update-slice_fusion.8.place) | copy-start | bytes 64
  111.3 26.6 %collective-permute-start.20 = (bf16[4,96,1536]{2,1,0:T(8,128)(2,1)S(1)}, bf16[4,96,1536]{2,1,0:T(8,128)(2,1)}, u32[]{:S(2)}, u32[]{:S(2)}) collective-permute-start(bf16[4,96,1536]{2,1,0:T(8,128)(2,1)S(1)} %pad_maximum_fusion.refs_0_), channel_id=1, source_target_pairs={{0,4},{4,0},{8,12},{12,8},{16,20},{20,16},{24,28},{28,24},{1,5},{5... | collective-permute-start | bytes 3538952 | tf_op jit(solution)/shard_map/ppermute | solution.py:470
  111.5 26.4 %collective-permute-start.21 = (bf16[4,96,1536]{2,1,0:T(8,128)(2,1)}, bf16[4,96,1536]{2,1,0:T(8,128)(2,1)}, u32[]{:S(2)}, u32[]{:S(2)}) collective-permute-start(bf16[4,96,1536]{2,1,0:T(8,128)(2,1)} %collective-permute-done.12.refs_2_), channel_id=1, source_target_pairs={{0,4},{4,0},{8,12},{12,8},{16,20},{20,16},{24,28},{28,24},{1,5},{5... | collective-permute-start | bytes 3538952 | tf_op jit(solution)/shard_map/ppermute | solution.py:470
  111.9 26.1 %collective-permute-start.22 = (bf16[4,96,1536]{2,1,0:T(8,128)(2,1)}, bf16[4,96,1536]{2,1,0:T(8,128)(2,1)}, u32[]{:S(2)}, u32[]{:S(2)}) collective-permute-start(bf16[4,96,1536]{2,1,0:T(8,128)(2,1)} %collective-permute-done.13.refs_4_), channel_id=1, source_target_pairs={{0,4},{4,0},{8,12},{12,8},{16,20},{20,16},{24,28},{28,24},{1,5},{5... | collective-permute-start | bytes 3538952 | tf_op jit(solution)/shard_map/ppermute | solution.py:470
  112.1 25.9 %collective-permute-start.23 = (bf16[4,96,1536]{2,1,0:T(8,128)(2,1)}, bf16[4,96,1536]{2,1,0:T(8,128)(2,1)}, u32[]{:S(2)}, u32[]{:S(2)}) collective-permute-start(bf16[4,96,1536]{2,1,0:T(8,128)(2,1)} %collective-permute-done.14.refs_6_), channel_id=1, source_target_pairs={{0,4},{4,0},{8,12},{12,8},{16,20},{20,16},{24,28},{28,24},{1,5},{5... | collective-permute-start | bytes 3538952 | tf_op jit(solution)/shard_map/ppermute | solution.py:470
  136.8 24.7 %copy-start.19 = (f32[8,768]{1,0:T(8,128)}, f32[8,768]{1,0:T(8,128)S(1)}, u32[]{:S(2)}) copy-start(f32[8,768]{1,0:T(8,128)S(1)} %bitcast_add_fusion) | copy-start | bytes 73732
  136.8 30.4 %collective-permute-start.19 = (bf16[4,96,1536]{2,1,0:T(8,128)(2,1)}, bf16[4,96,1536]{2,1,0:T(8,128)(2,1)S(1)}, u32[]{:S(2)}, u32[]{:S(2)}) collective-permute-start(bf16[4,96,1536]{2,1,0:T(8,128)(2,1)} %get-tuple-element.143), channel_id=1, source_target_pairs={{0,4},{4,0},{8,12},{12,8},{16,20},{20,16},{24,28},{28,24},{1,5},{5... | collective-permute-start | bytes 3538952 | tf_op jit(solution)/shard_map/ppermute | solution.py:470
  138.0 29.2 %copy-start.10 = (bf16[4,96,1536]{2,1,0:T(8,128)(2,1)S(1)}, bf16[4,96,1536]{2,1,0:T(8,128)(2,1)}, u32[]{:S(2)}) copy-start(bf16[4,96,1536]{2,1,0:T(8,128)(2,1)} %get-tuple-element.142) | copy-start | bytes 3538948
  161.5 41.2 %collective-permute-start.24 = (bf16[2,512,768]{2,1,0:T(8,128)(2,1)}, bf16[2,512,768]{2,1,0:T(8,128)(2,1)S(1)}, u32[]{:S(2)}, u32[]{:S(2)}) collective-permute-start(bf16[2,512,768]{2,1,0:T(8,128)(2,1)} %get-tuple-element.155), channel_id=1, source_target_pairs={{0,1},{1,0},{2,3},{3,2},{4,5},{5,4},{6,7},{7,6},{8,9},{9,8},{10,11... | collective-permute-start | bytes 4718600 | tf_op jit(solution)/shard_map/ppermute | solution.py:470
  167.6 26.9 %collective-permute-start.25 = (bf16[96,1536]{1,0:T(8,128)(2,1)S(1)}, bf16[96,1536]{1,0:T(8,128)(2,1)S(1)}, u32[]{:S(2)}, u32[]{:S(2)}) collective-permute-start(bf16[96,1536]{1,0:T(8,128)(2,1)S(1)} %get-tuple-element.216), channel_id=1, source_target_pairs={{0,8},{4,12},{8,0},{12,4},{16,24},{20,28},{24,16},{28,20},{1,9},{5... | collective-permute-start | bytes 884744 | tf_op jit(solution)/shard_map/ppermute | solution.py:470
  168.5 26.1 %collective-permute-start.26 = (bf16[96,1536]{1,0:T(8,128)(2,1)S(1)}, bf16[96,1536]{1,0:T(8,128)(2,1)S(1)}, u32[]{:S(2)}, u32[]{:S(2)}) collective-permute-start(bf16[96,1536]{1,0:T(8,128)(2,1)S(1)} %get-tuple-element.215), channel_id=1, source_target_pairs={{0,16},{4,20},{8,24},{12,28},{16,0},{20,4},{24,8},{28,12},{1,17},{... | collective-permute-start | bytes 884744 | tf_op jit(solution)/shard_map/ppermute | solution.py:470
  169.2 25.4 %collective-permute-start.27 = (bf16[96,1536]{1,0:T(8,128)(2,1)S(1)}, bf16[96,1536]{1,0:T(8,128)(2,1)S(1)}, u32[]{:S(2)}, u32[]{:S(2)}) collective-permute-start(bf16[96,1536]{1,0:T(8,128)(2,1)S(1)} %get-tuple-element.214), channel_id=1, source_target_pairs={{0,24},{4,28},{8,16},{12,20},{16,8},{20,12},{24,0},{28,4},{1,25},{... | collective-permute-start | bytes 884744 | tf_op jit(solution)/shard_map/ppermute | solution.py:470
  194.4 43.0 %collective-permute-start.28 = (bf16[2,512,768]{2,1,0:T(8,128)(2,1)}, bf16[2,512,768]{2,1,0:T(8,128)(2,1)}, u32[]{:S(2)}, u32[]{:S(2)}) collective-permute-start(bf16[2,512,768]{2,1,0:T(8,128)(2,1)} %get-tuple-element.164), channel_id=1, source_target_pairs={{0,1},{1,0},{2,3},{3,2},{4,5},{5,4},{6,7},{7,6},{8,9},{9,8},{10,11... | collective-permute-start | bytes 4718600 | tf_op jit(solution)/shard_map/ppermute | solution.py:470
  194.5 31.6 %copy-start.14 = (bf16[96,1536]{1,0:T(8,128)(2,1)}, bf16[96,1536]{1,0:T(8,128)(2,1)S(1)}, u32[]{:S(2)}) copy-start(bf16[96,1536]{1,0:T(8,128)(2,1)S(1)} %collective-permute-done.25) | copy-start | bytes 884740
  194.6 31.6 %copy-start.15 = (bf16[96,1536]{1,0:T(8,128)(2,1)}, bf16[96,1536]{1,0:T(8,128)(2,1)S(1)}, u32[]{:S(2)}) copy-start(bf16[96,1536]{1,0:T(8,128)(2,1)S(1)} %collective-permute-done.26) | copy-start | bytes 884740
  194.6 31.6 %copy-start.16 = (bf16[96,1536]{1,0:T(8,128)(2,1)}, bf16[96,1536]{1,0:T(8,128)(2,1)S(1)}, u32[]{:S(2)}) copy-start(bf16[96,1536]{1,0:T(8,128)(2,1)S(1)} %collective-permute-done.27) | copy-start | bytes 884740
  202.7 23.5 %copy-start.3 = (bf16[2,512,768]{2,1,0:T(8,128)(2,1)}, bf16[2,512,768]{2,1,0:T(8,128)(2,1)S(1)}, u32[]{:S(2)}) copy-start(bf16[2,512,768]{2,1,0:T(8,128)(2,1)S(1)} %collective-permute-done.24) | copy-start | bytes 4718596
  202.7 23.5 %copy-start.20 = (f32[8,768]{1,0:T(8,128)S(1)}, f32[8,768]{1,0:T(8,128)}, u32[]{:S(2)}) copy-start(f32[8,768]{1,0:T(8,128)} %get-tuple-element.177) | copy-start | bytes 73732
  202.7 23.5 %copy-start.21 = (f32[8,768]{1,0:T(8,128)S(1)}, f32[8,768]{1,0:T(8,128)}, u32[]{:S(2)}) copy-start(f32[8,768]{1,0:T(8,128)} %get-tuple-element.153) | copy-start | bytes 73732
  202.7 24.3 %slice-start.2 = ((f32[8,768]{1,0:T(8,128)}), f32[2,768]{1,0:T(2,128)S(1)}, s32[]{:S(2)}) async-start(f32[8,768]{1,0:T(8,128)} %copy-done.19), calls=%async_computation.2 | async-start | bytes 12288 | tf_op jit(solution)/shard_map/slice | solution.py:612
  227.4 13.2 %collective-permute-start.32 = (f32[12,768]{1,0:T(8,128)S(1)}, f32[12,768]{1,0:T(8,128)S(1)}, u32[]{:S(2)}, u32[]{:S(2)}) collective-permute-start(f32[12,768]{1,0:T(8,128)S(1)} %concatenate.61), channel_id=1, source_target_pairs={{0,4},{4,0},{8,12},{12,8},{16,20},{20,16},{24,28},{28,24},{1,5},{5... | collective-permute-start | bytes 110600 | tf_op jit(solution)/shard_map/ppermute | solution.py:470
  227.5 13.2 %collective-permute-start.30 = (bf16[4,96,3072]{2,1,0:T(8,128)(2,1)}, bf16[4,96,3072]{2,1,0:T(8,128)(2,1)S(1)}, u32[]{:S(2)}, u32[]{:S(2)}) collective-permute-start(bf16[4,96,3072]{2,1,0:T(8,128)(2,1)} %get-tuple-element.167), channel_id=1, source_target_pairs={{0,4},{4,0},{8,12},{12,8},{16,20},{20,16},{24,28},{28,24},{1,5},{5... | collective-permute-start | bytes 7077896 | tf_op jit(solution)/shard_map/ppermute | solution.py:470
  228.0 42.2 %collective-permute-start.29 = (bf16[2,512,768]{2,1,0:T(8,128)(2,1)}, bf16[2,512,768]{2,1,0:T(8,128)(2,1)}, u32[]{:S(2)}, u32[]{:S(2)}) collective-permute-start(bf16[2,512,768]{2,1,0:T(8,128)(2,1)} %get-tuple-element.165), channel_id=1, source_target_pairs={{0,1},{1,0},{2,3},{3,2},{4,5},{5,4},{6,7},{7,6},{8,9},{9,8},{10,11... | collective-permute-start | bytes 4718600 | tf_op jit(solution)/shard_map/ppermute | solution.py:470
  233.9 2.6 copy-start.6
  236.5 3.0 %copy-start.8 = (bf16[2,512,768]{2,1,0:T(8,128)(2,1)S(1)}, bf16[2,512,768]{2,1,0:T(8,128)(2,1)}, u32[]{:S(2)}) copy-start(bf16[2,512,768]{2,1,0:T(8,128)(2,1)} %get-tuple-element.165) | copy-start | bytes 4718596
  244.4 31.9 %collective-permute-start.33 = (bf16[104,3072]{1,0:T(8,128)(2,1)}, bf16[104,3072]{1,0:T(8,128)(2,1)S(1)}, u32[]{:S(2)}, u32[]{:S(2)}) collective-permute-start(bf16[104,3072]{1,0:T(8,128)(2,1)} %get-tuple-element.232), channel_id=1, source_target_pairs={{0,8},{4,12},{8,0},{12,4},{16,24},{20,28},{24,16},{28,20},{1,9},{5... | collective-permute-start | bytes 1916936 | tf_op jit(solution)/shard_map/ppermute | solution.py:470
  245.2 31.1 %collective-permute-start.34 = (bf16[104,3072]{1,0:T(8,128)(2,1)S(1)}, bf16[104,3072]{1,0:T(8,128)(2,1)S(1)}, u32[]{:S(2)}, u32[]{:S(2)}) collective-permute-start(bf16[104,3072]{1,0:T(8,128)(2,1)S(1)} %get-tuple-element.233), channel_id=1, source_target_pairs={{0,16},{4,20},{8,24},{12,28},{16,0},{20,4},{24,8},{28,12},{1,17},{... | collective-permute-start | bytes 1916936 | tf_op jit(solution)/shard_map/ppermute | solution.py:470
  245.9 30.4 %collective-permute-start.35 = (bf16[104,3072]{1,0:T(8,128)(2,1)S(1)}, bf16[104,3072]{1,0:T(8,128)(2,1)}, u32[]{:S(2)}, u32[]{:S(2)}) collective-permute-start(bf16[104,3072]{1,0:T(8,128)(2,1)S(1)} %get-tuple-element.234), channel_id=1, source_target_pairs={{0,24},{4,28},{8,16},{12,20},{16,8},{20,12},{24,0},{28,4},{1,25},{... | collective-permute-start | bytes 1916936 | tf_op jit(solution)/shard_map/ppermute | solution.py:470
  247.9 5.5 %slice-start = ((s8[4718592]{0:T(1024)(128)(4,1)}), s8[4194304]{0:T(1024)(128)(4,1)S(1)}, s32[]{:S(2)}) async-start(s8[4718592]{0:T(1024)(128)(4,1)} %bitcast.100), calls=%async_computation | async-start | bytes 8388608
  247.9 5.5 %slice-start.1 = ((s8[4718592]{0:T(1024)(128)(4,1)}), s8[524288]{0:T(1024)(128)(4,1)S(1)}, s32[]{:S(2)}) async-start(s8[4718592]{0:T(1024)(128)(4,1)} %bitcast.100), calls=%async_computation.1 | async-start | bytes 1048576
  248.0 5.5 %copy-start.2 = (bf16[2,512,768]{2,1,0:T(8,128)(2,1)S(1)}, bf16[2,512,768]{2,1,0:T(8,128)(2,1)}, u32[]{:S(2)}) copy-start(bf16[2,512,768]{2,1,0:T(8,128)(2,1)} %get-tuple-element.155) | copy-start | bytes 4718596
  248.0 26.7 %collective-permute-start.31 = (bf16[96,768]{1,0:T(8,128)(2,1)S(1)}, bf16[96,768]{1,0:T(8,128)(2,1)S(1)}, u32[]{:S(2)}, u32[]{:S(2)}) collective-permute-start(bf16[96,768]{1,0:T(8,128)(2,1)S(1)} %broadcast_select_fusion), channel_id=1, source_target_pairs={{0,1},{1,0},{2,3},{3,2},{4,5},{5,4},{6,7},{7,6},{8,9},{9,8},{10,11... | collective-permute-start | bytes 442376 | tf_op jit(solution)/shard_map/ppermute | solution.py:470
  278.1 3.8 %collective-permute-start.36 = (f32[12,96]{1,0:T(8,128)S(1)}, f32[12,96]{1,0:T(8,128)S(1)}, u32[]{:S(2)}, u32[]{:S(2)}) collective-permute-start(f32[12,96]{1,0:T(8,128)S(1)} %pad_maximum_fusion.5), channel_id=1, source_target_pairs={{0,1},{1,0},{2,3},{3,2},{4,5},{5,4},{6,7},{7,6},{8,9},{9,8},{10,11... | collective-permute-start | bytes 13832 | tf_op jit(solution)/shard_map/ppermute | solution.py:470
  280.1 7.8 %collective-permute-start.37 = (bf16[96,1536]{1,0:T(8,128)(2,1)S(1)}, bf16[96,1536]{1,0:T(8,128)(2,1)S(1)}, u32[]{:S(2)}, u32[]{:S(2)}) collective-permute-start(bf16[96,1536]{1,0:T(8,128)(2,1)S(1)} %pad_maximum_fusion.4), channel_id=1, source_target_pairs={{0,1},{1,0},{2,3},{3,2},{4,5},{5,4},{6,7},{7,6},{8,9},{9,8},{10,11... | collective-permute-start | bytes 884744 | tf_op jit(solution)/shard_map/ppermute | solution.py:470
  282.5 6.9 %copy-start.25 = (f32[96]{0:T(128)}, f32[96]{0:T(128)S(1)}, u32[]{:S(2)}) copy-start(f32[96]{0:T(128)S(1)} %get-tuple-element.267) | copy-start | bytes 1156
  (5 other events, 10.7 us)
